TPU v7x, 128 devices: a whole 4x4x4 slice. The times are simulated.
128 devices in a mesh: seq: 16 (over y, z), head: 8 (over x, core).
Axes of the slice: x: 4, y: 4, z: 4, core: 2. Of those that a mesh axis runs over, the one named last changes fastest.
Arguments:
- tile_tokens: bfloat16 [16, 8, 16, 128, 1536], P('seq', 'head'), may hold values from -6 to 6
- tile_gain: float32 [2, 1536], replicated, may hold values from 0.1 to 1.9
- tile_wq: bfloat16 [1536, 1536], P(('seq', 'head')), may hold values from -1.1875 to 1.1875
- tile_wkv: bfloat16 [1536, 3072], P(('seq', 'head')), may hold values from -1.1875 to 1.1875
- tile_wo: bfloat16 [1536, 1536], P(('seq', 'head')), may hold values from -0.15625 to 0.15625
- slide_proj: bfloat16 [1536, 768], replicated, may hold values from -0.15625 to 0.15625
- slide_cache: bfloat16 [16384, 768], P('seq'), may hold values from -6 to 6
- slide_gain: float32 [768], replicated, may hold values from 0.1 to 1.9
- slide_qkv: bfloat16 [3, 768, 768], P(None, None, 'head'), may hold values from -1.6875 to 1.6875
- send_map: int32 [8, 16, 16], replicated, may hold values from 0 to 1, as said below
Outputs:
- context: bfloat16 [16384, 768], P('seq', 'head')
- tile_output: bfloat16 [16, 8, 16, 128, 1536], P('seq', 'head')
Inputs may be any that keep to these rules, and one draw needn't show every extreme that they name: Entries are 0 or 1. For every h and d exactly 8 sources s have send_map[h, s, d] = 1; for every h some source has a 1 in every column.
All inputs are finite; a program needn't handle non-finite values.
Results may differ from a plain program's by a relative error of at most 0.022.
Values may be sent and summed in bfloat16 or wider, within the bound.
A program may use at most 128 MiB of HBM per device.

v0:
```python
import math

import jax
import jax.numpy as jnp
from jax import lax
from jax.sharding import PartitionSpec as P

TILE_HEAD_SIZE = 64
SLIDE_HEAD_SIZE = 48
RATE = 16


EPS = 1e-05


def norm_rows(values, gain):
    values = values.astype(jnp.float32)
    center = values - jnp.mean(values, axis=-1, keepdims=True)
    spread = jnp.mean(center * center, axis=-1, keepdims=True)
    return center * lax.rsqrt(spread + EPS) * gain


def encode_tiles(tile_block, tile_gain, w_query, w_pairs, w_out):
    length = tile_block.shape[1]
    features = tile_block.shape[2]
    head_count = features // TILE_HEAD_SIZE
    score_scale = 1.0 / math.sqrt(TILE_HEAD_SIZE)

    def one_tile(tile):
        normed = norm_rows(tile, tile_gain[0]).astype(jnp.bfloat16)
        key_value = jnp.dot(normed, w_pairs, preferred_element_type=jnp.float32).astype(
            jnp.bfloat16
        )
        query_rows = jnp.dot(normed, w_query, preferred_element_type=jnp.float32).astype(
            jnp.bfloat16
        )
        query_rows = query_rows.reshape(length, head_count, TILE_HEAD_SIZE)
        key_rows = key_value[:, :features].reshape(length, head_count, TILE_HEAD_SIZE)
        value_rows = key_value[:, features:].reshape(length, head_count, TILE_HEAD_SIZE)
        scores = (
            jnp.einsum("qhd,khd->hqk", query_rows, key_rows, preferred_element_type=jnp.float32)
            * score_scale
        )
        highest = jnp.max(scores, axis=2, keepdims=True)
        weights = jnp.exp(scores - highest)
        attention = (weights / jnp.sum(weights, axis=2, keepdims=True)).astype(jnp.bfloat16)
        context = jnp.einsum(
            "hqk,khd->qhd", attention, value_rows, preferred_element_type=jnp.float32
        ).astype(jnp.bfloat16)
        context = context.reshape(length, features)
        layer = (
            tile.astype(jnp.float32) + jnp.dot(context, w_out, preferred_element_type=jnp.float32)
        ).astype(jnp.bfloat16)
        embedded = norm_rows(layer[0], tile_gain[1]).astype(jnp.bfloat16)
        return (layer, embedded)

    return lax.map(one_tile, tile_block)


def partial_softmax(query_rows, key_rows, value_rows, score_scale):
    rows = query_rows.shape[0]
    block = min(512, rows)
    grouped = query_rows.reshape(rows // block, block, query_rows.shape[1], query_rows.shape[2])

    def one_block(block_rows):
        scores = (
            jnp.einsum("qhe,khe->hqk", block_rows, key_rows, preferred_element_type=jnp.float32)
            * score_scale
        )
        highest = jnp.max(scores, axis=2)
        weights = jnp.exp(scores - highest[:, :, None])
        totals = jnp.sum(weights, axis=2)
        numer = jnp.einsum(
            "hqk,khe->hqe",
            weights.astype(jnp.bfloat16),
            value_rows,
            preferred_element_type=jnp.float32,
        )
        return (highest, totals, numer)

    highest, totals, numer = lax.map(one_block, grouped)
    heads_here = query_rows.shape[1]
    highest = jnp.transpose(highest, (1, 0, 2)).reshape(heads_here, rows)
    totals = jnp.transpose(totals, (1, 0, 2)).reshape(heads_here, rows)
    numer = jnp.transpose(numer, (1, 0, 2, 3)).reshape(heads_here, rows, query_rows.shape[2])
    return (highest, totals, numer)


def combine_levels(near, far, offsets):
    near_top, near_total, near_numer = near
    far_top, far_total, far_numer = far
    rows = near_top.shape[1]
    phase = jnp.arange(rows, dtype=jnp.int32) % RATE
    picked = phase[None, :] == offsets[:, None]
    far_top_rows = jnp.repeat(far_top, RATE, axis=1)
    far_total_rows = jnp.repeat(far_total, RATE, axis=1)
    far_numer_rows = jnp.repeat(far_numer, RATE, axis=1)
    highest = jnp.where(picked, jnp.maximum(near_top, far_top_rows), near_top)
    near_factor = jnp.exp(near_top - highest)
    far_factor = jnp.where(picked, jnp.exp(jnp.minimum(far_top_rows - highest, 0.0)), 0.0)
    numer = near_numer * near_factor[:, :, None] + far_numer_rows * far_factor[:, :, None]
    totals = near_total * near_factor + far_total_rows * far_factor
    return numer / totals[:, :, None]


def per_device(
    tile_tokens,
    tile_gain,
    tile_wq,
    tile_wkv,
    tile_wo,
    slide_proj,
    slide_cache,
    slide_gain,
    slide_qkv,
    send_map,
):
    local_tiles = tile_tokens[0, 0]
    slot_count = local_tiles.shape[0]
    seq_count = lax.axis_size("seq")
    held_count = seq_count // 2
    seq_index = lax.axis_index("seq")
    head_index = lax.axis_index("head")
    w_query, w_pairs, w_out = (
        lax.all_gather(tile_wq, ("seq", "head"), axis=0, tiled=True),
        lax.all_gather(tile_wkv, ("seq", "head"), axis=0, tiled=True),
        lax.all_gather(tile_wo, ("seq", "head"), axis=0, tiled=True),
    )
    head_plan = lax.dynamic_index_in_dim(send_map, head_index, 0, keepdims=False)
    sent_flags = lax.dynamic_index_in_dim(head_plan, seq_index, 0, keepdims=False)
    sent_running = jnp.cumsum(sent_flags)
    places = jnp.arange(slot_count, dtype=jnp.int32)
    own_live = places < jnp.sum(sent_flags)
    target = jnp.minimum(
        jnp.sum((sent_running[None, :] <= places[:, None]).astype(jnp.int32), axis=1), seq_count - 1
    )
    before = jnp.minimum(sent_running - sent_flags, slot_count - 1)
    outgoing = jnp.where(
        sent_flags[:, None, None] > 0,
        jnp.take(local_tiles, before, axis=0),
        jnp.zeros((), jnp.bfloat16),
    )
    received = lax.all_to_all(outgoing, "seq", split_axis=0, concat_axis=0, tiled=True)
    incoming = lax.dynamic_index_in_dim(head_plan, seq_index, 1, keepdims=False)
    arrived = jnp.cumsum(incoming)
    ranks = jnp.arange(held_count, dtype=jnp.int32)
    source = jnp.minimum(
        jnp.sum((arrived[None, :] <= ranks[:, None]).astype(jnp.int32), axis=1), seq_count - 1
    )
    held_tiles = jnp.take(received, source, axis=0)
    layers, embedded = encode_tiles(held_tiles, tile_gain, w_query, w_pairs, w_out)
    position = jnp.clip(arrived - 1, 0, held_count - 1)
    arriving = incoming > 0
    out_layers = jnp.where(
        arriving[:, None, None], jnp.take(layers, position, axis=0), jnp.zeros((), jnp.bfloat16)
    )
    out_rows = jnp.where(
        arriving[:, None], jnp.take(embedded, position, axis=0), jnp.zeros((), jnp.bfloat16)
    )
    back_layers, back_rows = (
        lax.all_to_all(out_layers, "seq", split_axis=0, concat_axis=0, tiled=True),
        lax.all_to_all(out_rows, "seq", split_axis=0, concat_axis=0, tiled=True),
    )
    tile_layers = jnp.where(
        own_live[:, None, None], jnp.take(back_layers, target, axis=0), jnp.zeros((), jnp.bfloat16)
    )
    slot_rows = jnp.take(back_rows, target, axis=0)
    fresh = jnp.dot(slot_rows, slide_proj, preferred_element_type=jnp.float32).astype(jnp.bfloat16)
    shared = lax.all_gather(fresh[None], "head", axis=0, tiled=True)
    groups = shared.shape[0]
    slide_width = shared.shape[2]
    span = groups * slot_count
    row_plan = lax.dynamic_index_in_dim(send_map, seq_index, 1, keepdims=False)
    live_count = jnp.sum(row_plan, axis=1)
    live = (places[None, :] < live_count[:, None]).reshape(span)
    head_part = jnp.where(live[:, None], shared.reshape(span, slide_width), slide_cache[:span])
    slide_input = jnp.concatenate([head_part, slide_cache[span:]], axis=0)
    seq_rows = slide_input.shape[0]
    normed = norm_rows(slide_input, slide_gain).astype(jnp.bfloat16)
    projected = jnp.einsum(
        "tf,cfe->cte", normed, slide_qkv, preferred_element_type=jnp.float32
    ).astype(jnp.bfloat16)
    heads_here = slide_qkv.shape[2] // SLIDE_HEAD_SIZE
    query_rows = projected[0].reshape(seq_rows, heads_here, SLIDE_HEAD_SIZE)
    key_rows = projected[1].reshape(seq_rows, heads_here, SLIDE_HEAD_SIZE)
    value_rows = projected[2].reshape(seq_rows, heads_here, SLIDE_HEAD_SIZE)
    score_scale = 1.0 / math.sqrt(SLIDE_HEAD_SIZE)
    near = partial_softmax(query_rows, key_rows, value_rows, score_scale)
    offsets = (head_index * heads_here + jnp.arange(heads_here, dtype=jnp.int32)) % RATE
    selector = (offsets[:, None] == jnp.arange(RATE, dtype=jnp.int32)[None, :]).astype(jnp.bfloat16)

    def thin_rows(values):
        grouped = values.reshape(seq_rows // RATE, RATE, heads_here, SLIDE_HEAD_SIZE)
        return jnp.einsum(
            "rphe,hp->rhe", grouped, selector, preferred_element_type=jnp.float32
        ).astype(jnp.bfloat16)

    sparse_query = thin_rows(query_rows)
    all_keys, all_values = (
        lax.all_gather(thin_rows(key_rows), "seq", axis=0, tiled=True),
        lax.all_gather(thin_rows(value_rows), "seq", axis=0, tiled=True),
    )
    far = partial_softmax(sparse_query, all_keys, all_values, score_scale)
    merged = combine_levels(near, far, offsets)
    context = (
        jnp.transpose(merged, (1, 0, 2))
        .reshape(seq_rows, heads_here * SLIDE_HEAD_SIZE)
        .astype(jnp.bfloat16)
    )
    return (context, tile_layers[None, None])


def solution(mesh):
    return jax.shard_map(
        per_device,
        mesh=mesh,
        in_specs=(
            P("seq", "head", None, None, None),
            P(),
            P(("seq", "head"), None),
            P(("seq", "head"), None),
            P(("seq", "head"), None),
            P(),
            P("seq", None),
            P(),
            P(None, None, "head"),
            P(),
        ),
        out_specs=(P("seq", "head"), P("seq", "head", None, None, None)),
        check_vma=False,
    )
```

profile of v0, /device:TPU:0, one launch (start us, length us, event | category | flops | bytes accessed | tf_op | source)
XLA Modules:
  0.0 729.3 jit_solution(18131179794494552641)
XLA Ops:
  12.4 6.4 gather_fusion.4
  18.9 6.2 select_select_fusion.1
  25.1 8.2 %all-to-all-start = ((bf16[16,128,1536]{2,1,0:T(8,128)(2,1)}), bf16[16,128,1536]{2,1,0:T(8,128)(2,1)}, u32[]{:S(2)}, u32[]{:S(2)}) async-start(bf16[16,128,1536]{2,1,0:T(8,128)(2,1)} %select_select_fusion.1), calls=%async_computation | async-start | bytes 12582912 | tf_op jit(solution)/shard_map/all_to_all | solution.py:143
  44.2 99.0 %all-to-all-done = bf16[16,128,1536]{2,1,0:T(8,128)(2,1)} async-done(((bf16[16,128,1536]{2,1,0:T(8,128)(2,1)}), bf16[16,128,1536]{2,1,0:T(8,128)(2,1)}, u32[]{:S(2)}, u32[]{:S(2)}) %all-to-all-start) | async-done | bytes 6291488 | tf_op jit(solution)/shard_map/all_to_all | solution.py:143
  143.3 5.2 gather_fusion
  152.4 8.2 %reshape.506 = bf16[1536,1536]{1,0:T(8,128)(2,1)} reshape(bf16[128,12,1536]{2,1,0:T(8,128)(2,1)} %all-gather.10.cloned.1.call-done) | data formatting | bytes 9437184
  160.6 63.6 %all-gather.12.cloned.1.call-done = bf16[128,12,1536]{2,1,0:T(8,128)(2,1)} async-done(((bf16[1,12,1536]{2,1,0:T(8,128)(2,1)}), bf16[128,12,1536]{2,1,0:T(8,128)(2,1)}) %all-gather.12.cloned.1.call-update) | async-done | bytes 4718608 | tf_op jit(solution)/shard_map/all_gather | solution.py:127
  224.1 8.2 %reshape.508 = bf16[1536,1536]{1,0:T(8,128)(2,1)} reshape(bf16[128,12,1536]{2,1,0:T(8,128)(2,1)} %all-gather.12.cloned.1.call-done) | data formatting | bytes 9437184
  232.4 65.9 %all-gather.8.cloned.1.call-done = bf16[128,12,3072]{2,1,0:T(8,128)(2,1)} async-done(((bf16[1,12,3072]{2,1,0:T(8,128)(2,1)}), bf16[128,12,3072]{2,1,0:T(8,128)(2,1)}) %all-gather.8.cloned.1.call-update) | async-done | bytes 9437200 | tf_op jit(solution)/shard_map/all_gather | solution.py:126
  298.2 13.7 %reshape.504 = bf16[1536,3072]{1,0:T(8,128)(2,1)} reshape(bf16[128,12,3072]{2,1,0:T(8,128)(2,1)} %all-gather.8.cloned.1.call-done) | data formatting | bytes 18874368
  311.9 211.0 %while.9 = (s32[]{:T(128)}, bf16[8,128,1536]{2,1,0:T(8,128)(2,1)}, bf16[8,1536]{1,0:T(8,128)(2,1)}, bf16[8,128,1536]{2,1,0:T(8,128)(2,1)}, f32[2,1536]{1,0:T(2,1...) while((s32[]{:T(128)}, bf16[8,128,1536]{2,1,0:T(8,128)(2,1)}, ...), condition=%wide.region_12.14_spmd, body=%wide.region_5.13_spmd.sunk | while | flops 2523087616 | bytes 31931584 | solution.py:57
  315.0 5.3 convolution_convert_fusion.7
  329.7 4.0 bitcast_dynamic-update-slice_fusion.5
  341.4 5.3 convolution_convert_fusion.7
  367.8 5.3 convolution_convert_fusion.7
  394.2 5.3 convolution_convert_fusion.7
  420.5 5.3 convolution_convert_fusion.7
  446.9 5.3 convolution_convert_fusion.7
  461.6 4.0 bitcast_dynamic-update-slice_fusion.5
  473.3 5.3 convolution_convert_fusion.7
  499.6 5.3 convolution_convert_fusion.7
  522.9 5.7 gather_fusion.3
  531.2 6.6 all-to-all-start.1
  537.7 6.2 select_select_fusion.2
  545.4 5.9 all-to-all-start.2
  552.6 13.1 %all-gather = bf16[128,768]{1,0:T(8,128)(2,1)S(1)} all-gather(bf16[16,768]{1,0:T(8,128)(2,1)S(1)} %convolution_convert_fusion.3), channel_id=2, replica_groups=mesh['seq'=16,'head'=8] {'head'}, dimensions={0}, use_global_device_ids=true | all-gather | bytes 221184 | tf_op jit(solution)/shard_map/all_gather | solution.py:169
  572.5 5.0 multiply_reduce_fusion.4
  577.5 93.9 %all_gather.22 = bf16[1024,2,48]{2,1,0:T(2,128)(2,1)S(1)} all-gather(bf16[64,2,48]{2,1,0:T(2,128)(2,1)S(1)} %bitcast.173), channel_id=1, replica_groups=mesh['seq'=16,'head'=8] {'seq'}, dimensions={0}, use_global_device_ids=true | all-gather | bytes 208896 | tf_op jit(solution)/shard_map/all_gather | solution.py:200
  673.4 6.9 while.10
  682.1 24.4 %all_gather.23 = bf16[1024,2,48]{2,1,0:T(2,128)(2,1)S(1)} all-gather(bf16[64,2,48]{2,1,0:T(2,128)(2,1)S(1)} %bitcast.172), channel_id=1, replica_groups=mesh['seq'=16,'head'=8] {'seq'}, dimensions={0}, use_global_device_ids=true | all-gather | bytes 208896 | tf_op jit(solution)/shard_map/all_gather | solution.py:201
  710.0 6.6 gather_fusion.5
  716.5 6.2 fusion.31
  (282 shorter events, 196.2 us)
Async XLA Ops:
  7.2 544.9 %copy-start = (bf16[1536,768]{1,0:T(8,128)(2,1)S(1)}, bf16[1536,768]{1,0:T(8,128)(2,1)}, u32[]{:S(2)}) copy-start(bf16[1536,768]{1,0:T(8,128)(2,1)} %param.21) | copy-start | bytes 7077892
  7.2 145.2 %all-gather.10.cloned.1.call-start = ((), (), s32[]{:S(2)}) async-start(), calls=%async_computation.4 | async-start | bytes 6340608 | tf_op jit(solution)/shard_map/all_gather | solution.py:125
  7.9 216.2 %all-gather.12.cloned.1.call-start = ((), (), s32[]{:S(2)}) async-start(), calls=%async_computation.5 | async-start | bytes 6340608 | tf_op jit(solution)/shard_map/all_gather | solution.py:127
  8.7 289.6 %all-gather.8.cloned.1.call-start = ((), (), s32[]{:S(2)}) async-start(), calls=%async_computation.3 | async-start | bytes 12681216 | tf_op jit(solution)/shard_map/all_gather | solution.py:126
  25.1 118.1 %all-to-all-start = ((bf16[16,128,1536]{2,1,0:T(8,128)(2,1)}), bf16[16,128,1536]{2,1,0:T(8,128)(2,1)}, u32[]{:S(2)}, u32[]{:S(2)}) async-start(bf16[16,128,1536]{2,1,0:T(8,128)(2,1)} %select_select_fusion.1), calls=%async_computation | async-start | bytes 12582912 | tf_op jit(solution)/shard_map/all_to_all | solution.py:143
  37.8 110.7 %copy-start.19 = (s32[2]{0:T(128)}, s32[2]{0:T(128)S(1)}, u32[]{:S(2)}) copy-start(s32[2]{0:T(128)S(1)} %and_select_fusion) | copy-start | bytes 28
  522.9 5.7 copy-start.2
  522.9 6.4 copy-start.14
  522.9 6.4 copy-start.15
  531.2 14.2 %all-to-all-start.1 = ((bf16[16,2,768]{2,1,0:T(2,128)(2,1)}), bf16[16,2,768]{2,1,0:T(2,128)(2,1)S(1)}, u32[]{:S(2)}, u32[]{:S(2)}) async-start(bf16[16,2,768]{2,1,0:T(2,128)(2,1)} %reshape.527), calls=%async_computation.1 | async-start | bytes 98304 | tf_op jit(solution)/shard_map/all_to_all | solution.py:162
  544.0 8.1 %copy-start.16 = (pred[16]{0:T(512)(128)(4,1)S(1)}, pred[16]{0:T(512)(128)(4,1)}, u32[]{:S(2)}) copy-start(pred[16]{0:T(512)(128)(4,1)} %get-tuple-element.186) | copy-start | bytes 52
  545.4 164.6 %all-to-all-start.2 = ((bf16[16,128,1536]{2,1,0:T(8,128)(2,1)}), bf16[16,128,1536]{2,1,0:T(8,128)(2,1)}, u32[]{:S(2)}, u32[]{:S(2)}) async-start(bf16[16,128,1536]{2,1,0:T(8,128)(2,1)} %select_select_fusion.2), calls=%async_computation.2 | async-start | bytes 12582912 | tf_op jit(solution)/shard_map/all_to_all | solution.py:161
  551.3 14.4 %copy-start.21 = (pred[128]{0:T(512)(128)(4,1)S(1)}, pred[128]{0:T(512)(128)(4,1)}, u32[]{:S(2)}) copy-start(pred[128]{0:T(512)(128)(4,1)} %lt.115) | copy-start | bytes 388
  552.1 14.6 %copy-start.1 = (bf16[896,768]{1,0:T(8,128)(2,1)S(1)}, bf16[896,768]{1,0:T(8,128)(2,1)}, u32[]{:S(2)}) copy-start(bf16[896,768]{1,0:T(8,128)(2,1)} %slice.31) | copy-start | bytes 4128772
  552.1 15.5 %copy-start.22 = (bf16[3,768,96]{1,2,0:T(8,128)(2,1)S(1)}, bf16[3,768,96]{1,2,0:T(8,128)(2,1)}, u32[]{:S(2)}) copy-start(bf16[3,768,96]{1,2,0:T(8,128)(2,1)} %param.24) | copy-start | bytes 1327108
  552.1 15.5 %copy-start.23 = (f32[768]{0:T(1024)S(1)}, f32[768]{0:T(1024)}, u32[]{:S(2)}) copy-start(f32[768]{0:T(1024)} %param.23) | copy-start | bytes 9220
  568.6 3.9 copy-start.4
  671.8 1.4 copy-start.5
  673.3 8.8 %copy-start.3 = (bf16[2,64,48]{2,0,1:T(2,128)(2,1)S(1)}, bf16[2,64,48]{2,0,1:T(2,128)(2,1)}, u32[]{:S(2)}) copy-start(bf16[2,64,48]{2,0,1:T(2,128)(2,1)} %get-tuple-element.148) | copy-start | bytes 36868
  673.4 33.2 %copy-start.6 = (f32[2,64]{1,0:T(2,128)S(1)}, f32[2,64]{1,0:T(2,128)}, u32[]{:S(2)}) copy-start(f32[2,64]{1,0:T(2,128)} %copy-done.5) | copy-start | bytes 1540
  674.2 1.0 copy-start.11
  675.2 1.6 copy-start.9
  675.2 1.6 copy-start.12
  677.7 1.0 copy-start.11
  678.7 1.6 copy-start.9
  678.7 1.6 copy-start.12
  680.3 27.7 %copy-start.7 = (s32[1024]{0:T(1024)S(1)}, s32[1024]{0:T(1024)}, u32[]{:S(2)}) copy-start(s32[1024]{0:T(1024)} %add_select_fusion) | copy-start | bytes 12292
  680.3 27.7 %copy-start.10 = (f32[2,2,512]{2,1,0:T(2,128)S(1)}, f32[2,2,512]{2,1,0:T(2,128)}, u32[]{:S(2)}) copy-start(f32[2,2,512]{2,1,0:T(2,128)} %get-tuple-element.108) | copy-start | bytes 24580
  680.3 27.7 %copy-start.13 = (f32[2,2,512]{2,1,0:T(2,128)S(1)}, f32[2,2,512]{2,1,0:T(2,128)}, u32[]{:S(2)}) copy-start(f32[2,2,512]{2,1,0:T(2,128)} %get-tuple-element.109) | copy-start | bytes 24580
  680.3 27.7 %copy-start.20 = (s32[2]{0:T(128)S(1)}, s32[2]{0:T(128)}, u32[]{:S(2)}) copy-start(s32[2]{0:T(128)} %copy-done.19) | copy-start | bytes 28
  710.0 6.6 copy-start.17
  710.0 6.6 copy-start.18
  (2 other events, 1.9 us)
Sparse Core Ops, SparseCore 0:
  11.1 133.2 all-gather.9
  147.5 76.5 all-gather.11
  227.2 70.9 all-gather.7
where the time goes:
time: 734 us; the launch traced here: 729 us
  waiting for transfers between devices  232 us (32%)
  matrix products  145 us (20%)
  blocking collectives  131 us (18%)
  local copies, waits for them, and re-layouts  97.6 us (13%)
  other arithmetic  78.4 us (11%)
  starting transfers between devices  20.7 us (3%)
  between operations  14.2 us (2%)
  loops' own time  10.1 us (1%)
    all_to_all x1, waiting for transfers between devices, per_device(): lax.all_to_all(outgoing, 'seq', split_axis=0, concat_axis=0, tiled=True)  99 us
    all_gather x1, blocking collectives, per_device(): lax.all_gather(thin_rows(key_rows), 'seq', axis=0, tiled=True)  93.9 us
    all_gather x1, waiting for transfers between devices, per_device(): lax.all_gather(tile_wkv, ('seq', 'head'), axis=0, tiled=True)  65.9 us
    all_gather x1, waiting for transfers between devices, per_device(): lax.all_gather(tile_wo, ('seq', 'head'), axis=0, tiled=True)  63.6 us
    dot_general x8, matrix products, one_tile(): jnp.dot(normed, w_pairs, preferred_element_type=jnp.float32)  42.7 us
    dot_general x8, matrix products, one_tile(): jnp.dot(context, w_out, preferred_element_type=jnp.float32)  32.1 us
    unnamed x47, local copies, waits for them, and re-layouts  31.5 us
    dot_general x8, matrix products, one_tile(): jnp.dot(normed, w_query, preferred_element_type=jnp.float32)  26.4 us
  transfers between devices with their start and end apart: 6, of which 4 were waited for; matrix products, arithmetic and copies ran while one was open for 12% of the time, Pallas kernels for 0%

commit v1 on v0

v1 whole, which is shorter than its diff:
```python
import functools
import math

import jax
import jax.numpy as jnp
from jax import lax
from jax.experimental import pallas as pl
from jax.experimental.pallas import tpu as pltpu
from jax.sharding import PartitionSpec as P

TILE_HEAD_SIZE = 64
SLIDE_HEAD_SIZE = 48
RATE = 16
EPS = 1e-05
GROUP = 4
COLS = 512


def norm_rows(values, gain):
    values = values.astype(jnp.float32)
    center = values - jnp.mean(values, axis=-1, keepdims=True)
    spread = jnp.mean(center * center, axis=-1, keepdims=True)
    return center * lax.rsqrt(spread + EPS) * gain


def tile_kernel(live_ref, x_ref, gain_ref, wq_ref, wkv_ref, wo_ref, out_ref, emb_ref, xn, q, kv, ctx):
    step = pl.program_id(0)
    live = live_ref[0]
    tiles, length, width = x_ref.shape
    rows = tiles * length

    @pl.when(step * tiles < live)
    def _():
        for t in range(tiles):

            def norm(r, _):
                at = pl.ds(pl.multiple_of(r * 32, 32), 32)
                values = norm_rows(x_ref[t, at, :], gain_ref[0:1, :])
                xn[pl.ds(pl.multiple_of(t * length + r * 32, 32), 32), :] = values.astype(jnp.bfloat16)
                return 0

            lax.fori_loop(0, length // 32, norm, 0)

        def project(n, _):
            at = pl.ds(pl.multiple_of(n * COLS, COLS), COLS)
            q[:, at] = jnp.dot(xn[...], wq_ref[:, at], preferred_element_type=jnp.float32).astype(jnp.bfloat16)
            return 0

        lax.fori_loop(0, width // COLS, project, 0)

        def project_kv(n, _):
            at = pl.ds(pl.multiple_of(n * COLS, COLS), COLS)
            kv[:, at] = jnp.dot(xn[...], wkv_ref[:, at], preferred_element_type=jnp.float32).astype(jnp.bfloat16)
            return 0

        lax.fori_loop(0, 2 * width // COLS, project_kv, 0)

        lane = lax.broadcasted_iota(jnp.int32, (length, 128), 1)
        first = lane < TILE_HEAD_SIZE
        ones_a = jnp.where(first, 1.0, 0.0).astype(jnp.bfloat16)
        ones_b = jnp.where(first, 0.0, 1.0).astype(jnp.bfloat16)
        ones = jnp.concatenate([ones_a, ones_b], axis=0)
        scale = 1.0 / math.sqrt(TILE_HEAD_SIZE)

        def attend(p, _):
            at = pl.ds(pl.multiple_of(p * 128, 128), 128)
            vat = pl.ds(pl.multiple_of(width + p * 128, 128), 128)
            for t in range(tiles):
                tat = slice(t * length, (t + 1) * length)
                qp, kp, vp = q[tat, at], kv[tat, at], kv[tat, vat]
                keys = jnp.concatenate([kp * ones_a, kp * ones_b], axis=0)
                vals = jnp.concatenate([vp * ones_a, vp * ones_b], axis=0)
                vals = jnp.concatenate([vals, ones], axis=1)
                s = lax.dot_general(
                    qp, keys, (((1,), (1,)), ((), ())), preferred_element_type=jnp.float32
                )
                parts = []
                for half in range(2):
                    sh = s[:, half * length : (half + 1) * length]
                    top = jnp.max(sh, axis=1, keepdims=True)
                    parts.append(jnp.exp((sh - top) * scale).astype(jnp.bfloat16))
                w = jnp.concatenate(parts, axis=1)
                o = jnp.dot(w, vals, preferred_element_type=jnp.float32)
                ctx[tat, at] = (o[:, :128] / o[:, 128:]).astype(jnp.bfloat16)
            return 0

        lax.fori_loop(0, width // 128, attend, 0)

        def project_out(n, _):
            at = pl.ds(pl.multiple_of(n * COLS, COLS), COLS)
            y = jnp.dot(ctx[...], wo_ref[:, at], preferred_element_type=jnp.float32)
            for t in range(tiles):
                xt = x_ref[t, :, at].astype(jnp.float32)
                yt = xt + y[t * length : (t + 1) * length]
                out_ref[t, :, at] = jnp.where(step * tiles + t < live, yt, 0.0).astype(jnp.bfloat16)
            return 0

        lax.fori_loop(0, width // COLS, project_out, 0)
        for t in range(tiles):
            emb_ref[t] = norm_rows(out_ref[t, 0:16, :], gain_ref[1:2, :])[0:1]

    @pl.when(step * tiles >= live)
    def _():
        out_ref[...] = jnp.zeros_like(out_ref)
        emb_ref[...] = jnp.zeros_like(emb_ref)


def encode_tiles(live, tiles, gain, wq, wkv, wo):
    slots, length, width = tiles.shape
    rows = GROUP * length
    whole = pl.BlockSpec(memory_space=pltpu.VMEM)
    return pl.pallas_call(
        tile_kernel,
        grid_spec=pltpu.PrefetchScalarGridSpec(
            num_scalar_prefetch=1,
            grid=(slots // GROUP,),
            in_specs=[
                pl.BlockSpec((GROUP, length, width), lambda i, live: (i, 0, 0)),
                whole,
                whole,
                whole,
                whole,
            ],
            out_specs=[
                pl.BlockSpec((GROUP, length, width), lambda i, live: (i, 0, 0)),
                pl.BlockSpec((GROUP, 1, width), lambda i, live: (i, 0, 0)),
            ],
            scratch_shapes=[
                pltpu.VMEM((rows, width), jnp.bfloat16),
                pltpu.VMEM((rows, width), jnp.bfloat16),
                pltpu.VMEM((rows, 2 * width), jnp.bfloat16),
                pltpu.VMEM((rows, width), jnp.bfloat16),
            ],
        ),
        out_shape=[
            jax.ShapeDtypeStruct((slots, length, width), jnp.bfloat16),
            jax.ShapeDtypeStruct((slots, 1, width), jnp.float32),
        ],
        compiler_params=pltpu.CompilerParams(vmem_limit_bytes=56 * 1024 * 1024),
        name="tile_layer",
    )(live, tiles, gain, wq, wkv, wo)


def partial_softmax(query_rows, key_rows, value_rows, score_scale):
    rows = query_rows.shape[0]
    block = min(512, rows)
    grouped = query_rows.reshape(rows // block, block, query_rows.shape[1], query_rows.shape[2])

    def one_block(block_rows):
        scores = (
            jnp.einsum("qhe,khe->hqk", block_rows, key_rows, preferred_element_type=jnp.float32)
            * score_scale
        )
        highest = jnp.max(scores, axis=2)
        weights = jnp.exp(scores - highest[:, :, None])
        totals = jnp.sum(weights, axis=2)
        numer = jnp.einsum(
            "hqk,khe->hqe",
            weights.astype(jnp.bfloat16),
            value_rows,
            preferred_element_type=jnp.float32,
        )
        return (highest, totals, numer)

    highest, totals, numer = lax.map(one_block, grouped)
    heads_here = query_rows.shape[1]
    highest = jnp.transpose(highest, (1, 0, 2)).reshape(heads_here, rows)
    totals = jnp.transpose(totals, (1, 0, 2)).reshape(heads_here, rows)
    numer = jnp.transpose(numer, (1, 0, 2, 3)).reshape(heads_here, rows, query_rows.shape[2])
    return (highest, totals, numer)


def combine_levels(near, far, offsets):
    near_top, near_total, near_numer = near
    far_top, far_total, far_numer = far
    rows = near_top.shape[1]
    phase = jnp.arange(rows, dtype=jnp.int32) % RATE
    picked = phase[None, :] == offsets[:, None]
    far_top_rows = jnp.repeat(far_top, RATE, axis=1)
    far_total_rows = jnp.repeat(far_total, RATE, axis=1)
    far_numer_rows = jnp.repeat(far_numer, RATE, axis=1)
    highest = jnp.where(picked, jnp.maximum(near_top, far_top_rows), near_top)
    near_factor = jnp.exp(near_top - highest)
    far_factor = jnp.where(picked, jnp.exp(jnp.minimum(far_top_rows - highest, 0.0)), 0.0)
    numer = near_numer * near_factor[:, :, None] + far_numer_rows * far_factor[:, :, None]
    totals = near_total * near_factor + far_total_rows * far_factor
    return numer / totals[:, :, None]


def per_device(
    tile_tokens,
    tile_gain,
    tile_wq,
    tile_wkv,
    tile_wo,
    slide_proj,
    slide_cache,
    slide_gain,
    slide_qkv,
    send_map,
):
    local_tiles = tile_tokens[0, 0]
    slot_count = local_tiles.shape[0]
    seq_index = lax.axis_index("seq")
    head_index = lax.axis_index("head")
    w_query, w_pairs, w_out = (
        lax.all_gather(tile_wq, ("seq", "head"), axis=0, tiled=True),
        lax.all_gather(tile_wkv, ("seq", "head"), axis=0, tiled=True),
        lax.all_gather(tile_wo, ("seq", "head"), axis=0, tiled=True),
    )
    row_plan = lax.dynamic_index_in_dim(send_map, seq_index, 1, keepdims=False)
    live_count = jnp.sum(row_plan, axis=1)
    own_live = lax.dynamic_slice_in_dim(live_count, head_index, 1, 0)
    tile_layers, embedded = encode_tiles(own_live, local_tiles, tile_gain, w_query, w_pairs, w_out)
    slot_rows = embedded[:, 0].astype(jnp.bfloat16)
    fresh = jnp.dot(slot_rows, slide_proj, preferred_element_type=jnp.float32).astype(jnp.bfloat16)
    shared = lax.all_gather(fresh[None], "head", axis=0, tiled=True)
    groups = shared.shape[0]
    slide_width = shared.shape[2]
    span = groups * slot_count
    places = jnp.arange(slot_count, dtype=jnp.int32)
    live = (places[None, :] < live_count[:, None]).reshape(span)
    head_part = jnp.where(live[:, None], shared.reshape(span, slide_width), slide_cache[:span])
    slide_input = jnp.concatenate([head_part, slide_cache[span:]], axis=0)
    seq_rows = slide_input.shape[0]
    normed = norm_rows(slide_input, slide_gain).astype(jnp.bfloat16)
    projected = jnp.einsum(
        "tf,cfe->cte", normed, slide_qkv, preferred_element_type=jnp.float32
    ).astype(jnp.bfloat16)
    heads_here = slide_qkv.shape[2] // SLIDE_HEAD_SIZE
    query_rows = projected[0].reshape(seq_rows, heads_here, SLIDE_HEAD_SIZE)
    key_rows = projected[1].reshape(seq_rows, heads_here, SLIDE_HEAD_SIZE)
    value_rows = projected[2].reshape(seq_rows, heads_here, SLIDE_HEAD_SIZE)
    score_scale = 1.0 / math.sqrt(SLIDE_HEAD_SIZE)
    near = partial_softmax(query_rows, key_rows, value_rows, score_scale)
    offsets = (head_index * heads_here + jnp.arange(heads_here, dtype=jnp.int32)) % RATE
    selector = (offsets[:, None] == jnp.arange(RATE, dtype=jnp.int32)[None, :]).astype(jnp.bfloat16)

    def thin_rows(values):
        grouped = values.reshape(seq_rows // RATE, RATE, heads_here, SLIDE_HEAD_SIZE)
        return jnp.einsum(
            "rphe,hp->rhe", grouped, selector, preferred_element_type=jnp.float32
        ).astype(jnp.bfloat16)

    sparse_query = thin_rows(query_rows)
    both = jnp.concatenate([thin_rows(key_rows), thin_rows(value_rows)], axis=2)
    both = lax.all_gather(both, "seq", axis=0, tiled=True)
    far = partial_softmax(
        sparse_query, both[:, :, :SLIDE_HEAD_SIZE], both[:, :, SLIDE_HEAD_SIZE:], score_scale
    )
    merged = combine_levels(near, far, offsets)
    context = (
        jnp.transpose(merged, (1, 0, 2))
        .reshape(seq_rows, heads_here * SLIDE_HEAD_SIZE)
        .astype(jnp.bfloat16)
    )
    return (context, tile_layers[None, None])


def solution(mesh):
    return jax.shard_map(
        per_device,
        mesh=mesh,
        in_specs=(
            P("seq", "head", None, None, None),
            P(),
            P(("seq", "head"), None),
            P(("seq", "head"), None),
            P(("seq", "head"), None),
            P(),
            P("seq", None),
            P(),
            P(None, None, "head"),
            P(),
        ),
        out_specs=(P("seq", "head"), P("seq", "head", None, None, None)),
        check_vma=False,
    )
```

time: 734 us -> 402 us (0.55)
  matrix products: 145 us -> 6.9 us
  Pallas kernels: 0 us -> 94.7 us
  blocking collectives: 131 us -> 36.9 us
  other arithmetic: 78.4 us -> 11.5 us
  local copies, waits for them, and re-layouts: 97.6 us -> 40 us
  waiting for transfers between devices: 232 us -> 197 us
  starting transfers between devices: 20.7 us -> 0.11 us
  loops' own time: 10.1 us -> 0.02 us
    dot_general x32 -> x0, matrix products: 115 us -> none  [the longest x8 42.7 us: one_tile(): jnp.dot(normed, w_pairs, preferred_element_type=jnp.float32)]
    all_to_all x3 -> x0, waiting for transfers between devices: 100 us -> none  [the longest x1 99 us: per_device(): lax.all_to_all(outgoing, 'seq', split_axis=0, concat_axis=0, tiled=True)]
    pallas_call x0 -> x1, Pallas kernels: none -> 94.7 us  [encode_tiles(): pl.pallas_call(tile_kernel, grid_spec=pltpu.PrefetchScalarGridSpec(num_sc...]
    all_gather x2 -> x1, blocking collectives: 118 us -> 24.1 us  [per_device(): both = lax.all_gather(both, 'seq', axis=0, tiled=True)]
    all_gather x1, waiting for transfers between devices: 0.01 us -> 67.9 us  [per_device(): lax.all_gather(tile_wq, ('seq', 'head'), axis=0, tiled=True)]
    gather x6 -> x0, local copies, waits for them, and re-layouts: 25.3 us -> none  [the longest x1 6.56 us: per_device(): jnp.take(back_layers, target, axis=0)]
    sub x8 -> x0, matrix products: 22.8 us -> none  [one_tile(): weights = jnp.exp(scores - highest)]
    all_to_all x3 -> x0, starting transfers between devices: 20.6 us -> none  [the longest x1 8.18 us: per_device(): lax.all_to_all(outgoing, 'seq', split_axis=0, concat_axis=0, tiled=True)]
  transfers between devices with their start and end apart: 6 -> 3, of which waited for: 4 -> 3; matrix products, arithmetic and copies ran while one was open for 12% -> 5% of each run, Pallas kernels for 0% -> 0%
where the time goes in v1:
time: 402 us; the launch traced here: 401 us
  waiting for transfers between devices  197 us (49%)
  Pallas kernels  94.7 us (24%)
  local copies, waits for them, and re-layouts  40 us (10%)
  blocking collectives  36.9 us (9%)
  between operations  14 us (3%)
  other arithmetic  11.5 us (3%)
  matrix products  6.9 us (2%)
    pallas_call x1, Pallas kernels, encode_tiles(): pl.pallas_call(tile_kernel, grid_spec=pltpu.PrefetchScalarGridSpec(num_sc...  94.7 us
    all_gather x1, waiting for transfers between devices, per_device(): lax.all_gather(tile_wq, ('seq', 'head'), axis=0, tiled=True)  67.9 us
    all_gather x1, waiting for transfers between devices, per_device(): lax.all_gather(tile_wkv, ('seq', 'head'), axis=0, tiled=True)  65.9 us
    all_gather x1, waiting for transfers between devices, per_device(): lax.all_gather(tile_wo, ('seq', 'head'), axis=0, tiled=True)  60.8 us
    unnamed x16, local copies, waits for them, and re-layouts  30.2 us
    all_gather x1, blocking collectives, per_device(): both = lax.all_gather(both, 'seq', axis=0, tiled=True)  24.1 us
    all_gather x1, blocking collectives, per_device(): shared = lax.all_gather(fresh[None], 'head', axis=0, tiled=True)  12.8 us
  transfers between devices with their start and end apart: 3, of which 3 were waited for; matrix products, arithmetic and copies ran while one was open for 5% of the time, Pallas kernels for 0%

profile of v1, /device:TPU:0, one launch (start us, length us, event | category | flops | bytes accessed | tf_op | source)
XLA Modules:
  0.0 400.8 jit_solution(12181766208402873164)
XLA Ops:
  7.2 0.7 all-gather.8.cloned.1.call-update
  8.0 0.7 all-gather.12.cloned.1.call-update
  8.7 0.7 all-gather.10.cloned.1.call-update
  9.4 1.0 dynamic-slice_reduce_fusion
  10.4 0.6 dynamic_slice.15.live_ref
  11.2 2.5 slice.22
  13.9 67.9 %all-gather.8.cloned.1.call-done = bf16[128,12,1536]{2,1,0:T(8,128)(2,1)} async-done(((bf16[1,12,1536]{2,1,0:T(8,128)(2,1)}), bf16[128,12,1536]{2,1,0:T(8,128)(2,1)}) %all-gather.8.cloned.1.call-update) | async-done | bytes 4718608 | tf_op jit(solution)/shard_map/all_gather | solution.py:207
  81.8 8.2 %reshape.233.wq_ref = bf16[1536,1536]{1,0:T(8,128)(2,1)} reshape(bf16[128,12,1536]{2,1,0:T(8,128)(2,1)} %all-gather.8.cloned.1.call-done) | data formatting | bytes 9437184
  90.0 60.8 %all-gather.12.cloned.1.call-done = bf16[128,12,1536]{2,1,0:T(8,128)(2,1)} async-done(((bf16[1,12,1536]{2,1,0:T(8,128)(2,1)}), bf16[128,12,1536]{2,1,0:T(8,128)(2,1)}) %all-gather.12.cloned.1.call-update) | async-done | bytes 4718608 | tf_op jit(solution)/shard_map/all_gather | solution.py:209
  150.8 8.2 %reshape.237.wo_ref = bf16[1536,1536]{1,0:T(8,128)(2,1)} reshape(bf16[128,12,1536]{2,1,0:T(8,128)(2,1)} %all-gather.12.cloned.1.call-done) | data formatting | bytes 9437184
  159.0 65.9 %all-gather.10.cloned.1.call-done = bf16[128,12,3072]{2,1,0:T(8,128)(2,1)} async-done(((bf16[1,12,3072]{2,1,0:T(8,128)(2,1)}), bf16[128,12,3072]{2,1,0:T(8,128)(2,1)}) %all-gather.10.cloned.1.call-update) | async-done | bytes 9437200 | tf_op jit(solution)/shard_map/all_gather | solution.py:208
  224.9 13.7 %reshape.235.wkv_ref = bf16[1536,3072]{1,0:T(8,128)(2,1)} reshape(bf16[128,12,3072]{2,1,0:T(8,128)(2,1)} %all-gather.10.cloned.1.call-done) | data formatting | bytes 18874368
  238.6 94.7 %tile_layer.1 = (bf16[16,128,1536]{2,1,0:T(8,128)(2,1)}, f32[16,1,1536]{2,1,0:T(1,128)}) custom-call(s32[1]{0:T(128)} %dynamic_slice.15.live_ref, bf16[16,128,1536]{2,1,0:T(8,128)(2,1)} %bitcast.77, f32[2,1536]{1,0:T(2,128)} %gain_ref.1, bf16[1536,1536]{1,0:T(8,128)(2,1)} %reshape.233.wq_ref, bf16[1536,3072]{1,0:T(8,128)(2,1)} %reshape.235.wkv_ref, ...), custom_call_target="tpu_custom_call" | custom-call | tf_op jit(solution)/shard_map/tile_layer/pallas_call | solution.py:112
  333.3 1.1 convert_element_type.56
  334.8 12.8 %all-gather = bf16[128,768]{1,0:T(8,128)(2,1)S(1)} all-gather(bf16[16,768]{1,0:T(8,128)(2,1)S(1)} %convolution_convert_fusion), channel_id=2, replica_groups=mesh['seq'=16,'head'=8] {'head'}, dimensions={0}, use_global_device_ids=true | all-gather | bytes 221184 | tf_op jit(solution)/shard_map/all_gather | solution.py:217
  347.6 1.0 slice_select_fusion
  348.9 0.6 fusion.17
  349.6 0.9 fusion.20
  350.8 0.8 reshape_reshape_squeeze.12
  352.7 3.1 multiply_reduce_fusion.3
  355.9 24.1 %all_gather.19 = bf16[1024,2,96]{2,1,0:T(2,128)(2,1)S(1)} all-gather(bf16[64,2,96]{2,1,0:T(2,128)(2,1)S(1)} %pad_maximum_fusion.2), channel_id=1, replica_groups=mesh['seq'=16,'head'=8] {'seq'}, dimensions={0}, use_global_device_ids=true | all-gather | bytes 417792 | tf_op jit(solution)/shard_map/all_gather | solution.py:247
  380.0 0.9 fusion.42
  382.0 6.8 %while.2 = (s32[]{:T(128)}, f32[2,2,512]{2,1,0:T(2,128)S(1)}, f32[2,2,512]{2,1,0:T(2,128)S(1)}, f32[2,2,512,48]{2,3,1,0:T(8,128)}, bf16[2,512,2,48]{1,3,2,0:T(8,...) while((s32[]{:T(128)}, f32[2,2,512]{2,1,0:T(2,128)S(1)}, ...), condition=%wide.region_6.7_spmd, body=%wide.region_3.6_spmd.sunk | while | flops 209713152 | bytes 13304413 | solution.py:165
  382.0 0.8 multiply_reduce_fusion.5
  382.8 0.9 fusion.56
  383.8 1.6 fusion.57
  385.4 0.8 multiply_reduce_fusion.5
  386.2 0.9 fusion.56
  387.2 1.6 fusion.57
  389.0 1.9 copy.54
  391.2 1.1 copy.28
  392.4 1.9 divide_convert_fusion
  (50 shorter events, 4.3 us)
Async XLA Ops:
  7.2 327.2 %copy-start = (bf16[1536,768]{1,0:T(8,128)(2,1)S(1)}, bf16[1536,768]{1,0:T(8,128)(2,1)}, u32[]{:S(2)}) copy-start(bf16[1536,768]{1,0:T(8,128)(2,1)} %param.17) | copy-start | bytes 7077892
  7.2 74.7 %all-gather.8.cloned.1.call-start = ((), (), s32[]{:S(2)}) async-start(), calls=%async_computation | async-start | bytes 6340608 | tf_op jit(solution)/shard_map/all_gather | solution.py:207
  7.9 142.9 %all-gather.12.cloned.1.call-start = ((), (), s32[]{:S(2)}) async-start(), calls=%async_computation.2 | async-start | bytes 6340608 | tf_op jit(solution)/shard_map/all_gather | solution.py:209
  8.7 216.3 %all-gather.10.cloned.1.call-start = ((), (), s32[]{:S(2)}) async-start(), calls=%async_computation.1 | async-start | bytes 12681216 | tf_op jit(solution)/shard_map/all_gather | solution.py:208
  333.3 15.3 %copy-start.2 = (bf16[896,768]{1,0:T(8,128)(2,1)S(1)}, bf16[896,768]{1,0:T(8,128)(2,1)}, u32[]{:S(2)}) copy-start(bf16[896,768]{1,0:T(8,128)(2,1)} %slice.22) | copy-start | bytes 4128772
  334.4 15.2 %copy-start.4 = (bf16[3,768,96]{1,2,0:T(8,128)(2,1)S(1)}, bf16[3,768,96]{1,2,0:T(8,128)(2,1)}, u32[]{:S(2)}) copy-start(bf16[3,768,96]{1,2,0:T(8,128)(2,1)} %param.20) | copy-start | bytes 1327108
  334.4 15.2 %copy-start.5 = (f32[768]{0:T(1024)S(1)}, f32[768]{0:T(1024)}, u32[]{:S(2)}) copy-start(f32[768]{0:T(1024)} %param.19) | copy-start | bytes 9220
  352.7 29.2 %copy-start.3 = (bf16[2,512,2,48]{1,0,3,2:T(2,128)(2,1)S(1)}, bf16[2,512,2,48]{1,0,3,2:T(2,128)(2,1)}, u32[]{:S(2)}) copy-start(bf16[2,512,2,48]{1,0,3,2:T(2,128)(2,1)} %reshape_reshape_squeeze.12) | copy-start | bytes 589828
  388.8 5.5 %copy-start.1 = (bf16[1536,768]{1,0:T(8,128)(2,1)S(1)}, bf16[1536,768]{1,0:T(8,128)(2,1)}, u32[]{:S(2)}) copy-start(bf16[1536,768]{1,0:T(8,128)(2,1)} %param.17) | copy-start | bytes 7077892
Sparse Core Ops, SparseCore 0:
  11.1 70.6 all-gather.7
  84.9 65.8 all-gather.11
  153.9 70.9 all-gather.9

commit v2 on v1

--- a/solution.py
+++ b/solution.py
@@ -1,4 +1,3 @@
-import functools
 import math
 
 import jax
@@ -14,6 +13,201 @@
 EPS = 1e-05
 GROUP = 4
 COLS = 512
+MESH = pl.DeviceIdType.MESH
+ORDERS = (("x", "y", "z"), ("y", "z", "x"), ("z", "x", "y"))
+RING = 4
+
+
+class Place:
+    def __init__(self):
+        seq, head = lax.axis_index("seq"), lax.axis_index("head")
+        self.core = head % 2
+        self.at = {"x": head // 2, "y": seq // RING, "z": seq % RING}
+
+    def device(self, axis=None, shift=0, core=None):
+        at = dict(self.at)
+        if axis is not None:
+            at[axis] = (at[axis] + shift) % RING
+        core = self.core if core is None else core
+        return (at["y"] * RING + at["z"], at["x"] * 2 + core)
+
+    def index(self, matrix, core, part, phase, shift):
+        order = ORDERS[part]
+        at = {}
+        for number, axis in enumerate(order):
+            if number < phase:
+                at[axis] = None
+            elif number == phase:
+                at[axis] = (self.at[axis] + shift) % RING
+            else:
+                at[axis] = self.at[axis]
+        every = slice(None)
+        x, y, z = at["x"], at["y"], at["z"]
+        low, high = (every, every) if x is None else (x % 2, x // 2)
+        return (
+            matrix,
+            low,
+            core,
+            part,
+            every if y is None else y,
+            every if z is None else z,
+            high,
+        )
+
+
+def gather_kernel(w_ref, full, inbox, own, swap_send, swap_recv, send, recv, pair_send, pair_recv, keep):
+    here = Place()
+    core, other = here.core, 1 - here.core
+    x = here.at["x"]
+    low = x % 2
+    mate = x + 1 - 2 * low
+    spot = here.device()[0]
+    members = [(spot, x * 2 + other), (spot, mate * 2 + core), (spot, mate * 2 + other)]
+    me = 2 * low + core
+    ids = [2 * low + other, 2 * (1 - low) + core, 2 * (1 - low) + other]
+
+    barrier = pltpu.get_barrier_semaphore()
+    partners = [here.device(a, s) for a in "xyz" for s in (1, 3)] + [members[0], members[2]]
+    for partner in partners:
+        pl.semaphore_signal(barrier, inc=1, device_id=partner, device_id_type=MESH)
+    pl.semaphore_wait(barrier, len(partners))
+
+    swaps = []
+    for n in range(3):
+        swaps.append(
+            pltpu.make_async_remote_copy(
+                src_ref=w_ref.at[ids[n]],
+                dst_ref=inbox.at[n],
+                send_sem=swap_send.at[n],
+                recv_sem=swap_recv.at[n],
+                device_id=members[n],
+                device_id_type=MESH,
+            )
+        )
+        swaps[n].start()
+    for n in range(3):
+        swaps[n].wait_recv()
+    count = 4 * 48
+    row = lax.broadcasted_iota(jnp.int32, (count, count), 0)
+    col = lax.broadcasted_iota(jnp.int32, (count, count), 1)
+    matrix, member, inner = row // 48, (row % 48) // 12, row % 12
+    total = None
+    sources = [w_ref[me]] + [inbox[n] for n in range(3)]
+    names = [me] + ids
+    for piece, name in zip(sources, names):
+        want = matrix * 12 + inner
+        pick = jnp.where((member == name) & (want == col), 1.0, 0.0).astype(jnp.bfloat16)[:, :48]
+        term = jnp.dot(pick, piece, preferred_element_type=jnp.float32)
+        total = term if total is None else total + term
+    for m in range(4):
+        for p in range(3):
+            own[m, p] = total[m * 48 : (m + 1) * 48, p * 128 : (p + 1) * 128].astype(jnp.bfloat16)
+
+    def move(m, p, phase, piece, origin, target):
+        spots = here.index(m, core, p, phase, origin)
+        axis = ORDERS[p][phase]
+        src = own.at[m, p] if phase == 0 and origin == 0 else full.at[spots]
+        return pltpu.make_async_remote_copy(
+            src_ref=src,
+            dst_ref=full.at[spots],
+            send_sem=send.at[m, p, phase, piece],
+            recv_sem=recv.at[m, p, phase, piece],
+            device_id=here.device(axis, target),
+            device_id_type=MESH,
+        )
+
+    def arrive(m, p, phase, piece, origin):
+        spots = here.index(m, core, p, phase, origin)
+        axis = ORDERS[p][phase]
+        pltpu.make_async_remote_copy(
+            src_ref=full.at[spots],
+            dst_ref=full.at[spots],
+            send_sem=send.at[m, p, phase, piece],
+            recv_sem=recv.at[m, p, phase, piece],
+            device_id=here.device(axis, 1),
+            device_id_type=MESH,
+        ).wait_recv()
+
+    def pair(m, p, piece, phase, origin, side):
+        spots = here.index(m, side, p, phase, origin)
+        return pltpu.make_async_remote_copy(
+            src_ref=full.at[spots],
+            dst_ref=full.at[spots],
+            send_sem=pair_send.at[m, p, piece],
+            recv_sem=pair_recv.at[m, p, piece],
+            device_id=members[0],
+            device_id_type=MESH,
+        )
+
+    sent = []
+
+    def go(copy):
+        copy.start()
+        sent.append(copy)
+
+    todo = [(m, p) for m in range(4) for p in range(3)]
+    keeps = []
+    for m, p in todo:
+        go(move(m, p, 0, 0, 0, 1))
+        go(move(m, p, 0, 1, 0, 3))
+    for m, p in todo:
+        copy = pltpu.make_async_copy(own.at[m, p], full.at[here.index(m, core, p, 0, 0)], keep.at[m, p])
+        copy.start()
+        keeps.append(copy)
+    for copy in keeps:
+        copy.wait()
+    for phase in range(3):
+        for m, p in todo:
+            arrive(m, p, phase, 0, 3)
+            arrive(m, p, phase, 1, 1)
+            if m % 2 == 0:
+                go(move(m, p, phase, 2, 3, 1))
+            else:
+                go(move(m, p, phase, 2, 1, 3))
+            if phase == 2:
+                go(pair(m, p, 1, 2, 3, core))
+                go(pair(m, p, 2, 2, 1, core))
+        for m, p in todo:
+            arrive(m, p, phase, 2, 2)
+            if phase < 2:
+                go(move(m, p, phase + 1, 0, 0, 1))
+                go(move(m, p, phase + 1, 1, 0, 3))
+            if phase == 1:
+                go(pair(m, p, 0, 2, 0, core))
+            if phase == 2:
+                go(pair(m, p, 3, 2, 2, core))
+    for m, p in todo:
+        for piece, origin in enumerate((0, 3, 1, 2)):
+            pair(m, p, piece, 2, origin, other).wait_recv()
+    for copy in swaps + sent:
+        copy.wait_send()
+
+
+def gather_weights(wq, wkv, wo):
+    rows, width = wq.shape
+    parts = jnp.concatenate([wkv, wq, wo], axis=1)
+    parts = parts.reshape(rows, 4, 4, width // 4)
+    parts = jnp.transpose(parts, (2, 1, 0, 3)).reshape(4, 4 * rows, width // 4)
+    dma = pltpu.SemaphoreType.DMA
+    return pl.pallas_call(
+        gather_kernel,
+        in_specs=[pl.BlockSpec(memory_space=pltpu.VMEM)],
+        out_specs=pl.BlockSpec(memory_space=pl.ANY),
+        out_shape=jax.ShapeDtypeStruct((4, 2, 2, 3, 4, 4, 2, 48, 128), jnp.bfloat16),
+        scratch_shapes=[
+            pltpu.VMEM((3, 48, 384), jnp.bfloat16),
+            pltpu.VMEM((4, 3, 48, 128), jnp.bfloat16),
+            dma((3,)),
+            dma((3,)),
+            dma((4, 3, 3, 3)),
+            dma((4, 3, 3, 3)),
+            dma((4, 3, 4)),
+            dma((4, 3, 4)),
+            dma((4, 3)),
+        ],
+        compiler_params=pltpu.CompilerParams(collective_id=0, has_side_effects=True, vmem_limit_bytes=40 * 1024 * 1024),
+        name="weight_gather",
+    )(parts)
 
 
 def norm_rows(values, gain):
@@ -23,11 +217,25 @@
     return center * lax.rsqrt(spread + EPS) * gain
 
 
-def tile_kernel(live_ref, x_ref, gain_ref, wq_ref, wkv_ref, wo_ref, out_ref, emb_ref, xn, q, kv, ctx):
+def tile_kernel(live_ref, x_ref, gain_ref, w_ref, out_ref, emb_ref, w, xn, q, kv, ctx, load):
     step = pl.program_id(0)
     live = live_ref[0]
     tiles, length, width = x_ref.shape
-    rows = tiles * length
+    blocks = COLS // 128
+    loads = [pltpu.make_async_copy(w_ref.at[m], w.at[m], load.at[m]) for m in range(4)]
+
+    @pl.when(step == 0)
+    def _():
+        for copy in loads:
+            copy.start()
+
+    def ready(m):
+        @pl.when(step == 0)
+        def _():
+            loads[m].wait()
+
+    def columns(m, n):
+        return jnp.concatenate([w[m, n * blocks + j] for j in range(blocks)], axis=1)
 
     @pl.when(step * tiles < live)
     def _():
@@ -41,19 +249,17 @@
 
             lax.fori_loop(0, length // 32, norm, 0)
 
-        def project(n, _):
-            at = pl.ds(pl.multiple_of(n * COLS, COLS), COLS)
-            q[:, at] = jnp.dot(xn[...], wq_ref[:, at], preferred_element_type=jnp.float32).astype(jnp.bfloat16)
-            return 0
-
-        lax.fori_loop(0, width // COLS, project, 0)
-
-        def project_kv(n, _):
-            at = pl.ds(pl.multiple_of(n * COLS, COLS), COLS)
-            kv[:, at] = jnp.dot(xn[...], wkv_ref[:, at], preferred_element_type=jnp.float32).astype(jnp.bfloat16)
-            return 0
-
-        lax.fori_loop(0, 2 * width // COLS, project_kv, 0)
+        for m, ref, base in ((0, kv, 0), (1, kv, width), (2, q, 0)):
+            ready(m)
+
+            def project(n, _):
+                at = pl.ds(pl.multiple_of(base + n * COLS, COLS), COLS)
+                ref[:, at] = jnp.dot(
+                    xn[...], columns(m, n), preferred_element_type=jnp.float32
+                ).astype(jnp.bfloat16)
+                return 0
+
+            lax.fori_loop(0, width // COLS, project, 0)
 
         lane = lax.broadcasted_iota(jnp.int32, (length, 128), 1)
         first = lane < TILE_HEAD_SIZE
@@ -86,9 +292,11 @@
 
         lax.fori_loop(0, width // 128, attend, 0)
 
+        ready(3)
+
         def project_out(n, _):
             at = pl.ds(pl.multiple_of(n * COLS, COLS), COLS)
-            y = jnp.dot(ctx[...], wo_ref[:, at], preferred_element_type=jnp.float32)
+            y = jnp.dot(ctx[...], columns(3, n), preferred_element_type=jnp.float32)
             for t in range(tiles):
                 xt = x_ref[t, :, at].astype(jnp.float32)
                 yt = xt + y[t * length : (t + 1) * length]
@@ -101,11 +309,13 @@
 
     @pl.when(step * tiles >= live)
     def _():
+        for m in range(4):
+            ready(m)
         out_ref[...] = jnp.zeros_like(out_ref)
         emb_ref[...] = jnp.zeros_like(emb_ref)
 
 
-def encode_tiles(live, tiles, gain, wq, wkv, wo):
+def encode_tiles(live, tiles, gain, weights):
     slots, length, width = tiles.shape
     rows = GROUP * length
     whole = pl.BlockSpec(memory_space=pltpu.VMEM)
@@ -117,19 +327,19 @@
             in_specs=[
                 pl.BlockSpec((GROUP, length, width), lambda i, live: (i, 0, 0)),
                 whole,
-                whole,
-                whole,
-                whole,
+                pl.BlockSpec(memory_space=pl.ANY),
             ],
             out_specs=[
                 pl.BlockSpec((GROUP, length, width), lambda i, live: (i, 0, 0)),
                 pl.BlockSpec((GROUP, 1, width), lambda i, live: (i, 0, 0)),
             ],
             scratch_shapes=[
+                pltpu.VMEM((4, width // 128, width, 128), jnp.bfloat16),
                 pltpu.VMEM((rows, width), jnp.bfloat16),
                 pltpu.VMEM((rows, width), jnp.bfloat16),
                 pltpu.VMEM((rows, 2 * width), jnp.bfloat16),
                 pltpu.VMEM((rows, width), jnp.bfloat16),
+                pltpu.SemaphoreType.DMA((4,)),
             ],
         ),
         out_shape=[
@@ -138,7 +348,7 @@
         ],
         compiler_params=pltpu.CompilerParams(vmem_limit_bytes=56 * 1024 * 1024),
         name="tile_layer",
-    )(live, tiles, gain, wq, wkv, wo)
+    )(live, tiles, gain, weights)
 
 
 def partial_softmax(query_rows, key_rows, value_rows, score_scale):
@@ -203,15 +413,13 @@
     slot_count = local_tiles.shape[0]
     seq_index = lax.axis_index("seq")
     head_index = lax.axis_index("head")
-    w_query, w_pairs, w_out = (
-        lax.all_gather(tile_wq, ("seq", "head"), axis=0, tiled=True),
-        lax.all_gather(tile_wkv, ("seq", "head"), axis=0, tiled=True),
-        lax.all_gather(tile_wo, ("seq", "head"), axis=0, tiled=True),
-    )
+    weights = gather_weights(tile_wq, tile_wkv, tile_wo)
+    width = local_tiles.shape[2]
+    weights = weights.reshape(4, width // 128, width, 128)
     row_plan = lax.dynamic_index_in_dim(send_map, seq_index, 1, keepdims=False)
     live_count = jnp.sum(row_plan, axis=1)
     own_live = lax.dynamic_slice_in_dim(live_count, head_index, 1, 0)
-    tile_layers, embedded = encode_tiles(own_live, local_tiles, tile_gain, w_query, w_pairs, w_out)
+    tile_layers, embedded = encode_tiles(own_live, local_tiles, tile_gain, weights)
     slot_rows = embedded[:, 0].astype(jnp.bfloat16)
     fresh = jnp.dot(slot_rows, slide_proj, preferred_element_type=jnp.float32).astype(jnp.bfloat16)
     shared = lax.all_gather(fresh[None], "head", axis=0, tiled=True)

time: 402 us -> 222 us (0.55)
  waiting for transfers between devices: 197 us -> 0 us
  blocking collectives: 36.9 us -> 111 us
  Pallas kernels: 94.7 us -> 69.8 us
  local copies, waits for them, and re-layouts: 40 us -> 17.1 us
  between operations: 14 us -> 0.87 us
    all_gather x3 -> x0, waiting for transfers between devices: 195 us -> none  [the longest x1 67.9 us: per_device(): lax.all_gather(tile_wq, ('seq', 'head'), axis=0, tiled=True)]
    pallas_call x1, Pallas kernels: 94.7 us -> 13 us  [encode_tiles(): pl.pallas_call(tile_kernel, grid_spec=pltpu.PrefetchScalarGridSpec(num_sc...]
    all_gather x1, blocking collectives: 12.8 us -> 86.8 us  [per_device(): shared = lax.all_gather(fresh[None], 'head', axis=0, tiled=True)]
    pallas_call x0 -> x1, Pallas kernels: none -> 56.8 us  [gather_weights(): pl.pallas_call(gather_kernel, in_specs=[pl.BlockSpec(memory_space=pltpu.V...]
    unnamed x16 -> x7, local copies, waits for them, and re-layouts: 30.2 us -> 0.11 us
    another operation x3, local copies, waits for them, and re-layouts: 0.74 us -> 5.19 us  [thin_rows(): values.reshape(seq_rows // RATE, RATE, heads_here, SLIDE_HEAD_SIZE)]
  transfers between devices with their start and end apart: 3 -> 0, of which waited for: 3 -> 0; matrix products, arithmetic and copies ran while one was open for 5% -> 0% of each run, Pallas kernels for 0% -> 0%
where the time goes in v2:
time: 222 us; the launch traced here: 221 us
  blocking collectives  111 us (50%)
  Pallas kernels  69.8 us (31%)
  local copies, waits for them, and re-layouts  17.1 us (8%)
  other arithmetic  13.8 us (6%)
  matrix products  8.97 us (4%)
    all_gather x1, blocking collectives, per_device(): shared = lax.all_gather(fresh[None], 'head', axis=0, tiled=True)  86.8 us
    pallas_call x1, Pallas kernels, gather_weights(): pl.pallas_call(gather_kernel, in_specs=[pl.BlockSpec(memory_space=pltpu.V...  56.8 us
    all_gather x1, blocking collectives, per_device(): both = lax.all_gather(both, 'seq', axis=0, tiled=True)  23.9 us
    pallas_call x1, Pallas kernels, encode_tiles(): pl.pallas_call(tile_kernel, grid_spec=pltpu.PrefetchScalarGridSpec(num_sc...  13 us
    another operation x3, local copies, waits for them, and re-layouts, thin_rows(): values.reshape(seq_rows // RATE, RATE, heads_here, SLIDE_HEAD_SIZE)  5.19 us
    dot_general x3, matrix products, one_block(): jnp.einsum('hqk,khe->hqe', weights.astype(jnp.bfloat16), value_rows, pref...  4.52 us

profile of v2, /device:TPU:0, one launch (start us, length us, event | category | flops | bytes accessed | tf_op | source)
XLA Modules:
  0.0 221.3 jit_solution(5978697375890077387)
XLA Ops:
  0.7 1.1 dynamic-slice_reduce_fusion
  2.4 1.0 pad_maximum_fusion.2
  3.6 56.8 %weight_gather.1 = bf16[4,2,2,3,4,4,2,48,128]{8,7,6,5,4,3,2,1,0:T(8,128)(2,1)} custom-call(bf16[4,48,384]{2,1,0:T(8,128)(2,1)S(1)} %copy.24.w_ref), custom_call_target="tpu_custom_call" | custom-call | tf_op jit(solution)/shard_map/weight_gather/pallas_call | solution.py:192
  60.4 13.0 %tile_layer.1 = (bf16[16,128,1536]{2,1,0:T(8,128)(2,1)}, f32[16,1,1536]{2,1,0:T(1,128)}) custom-call(s32[1]{0:T(128)} %dynamic_slice.15.live_ref, bf16[16,128,1536]{2,1,0:T(8,128)(2,1)} %bitcast.79, f32[2,1536]{1,0:T(2,128)} %gain_ref.1, bf16[4,12,1536,128]{3,2,1,0:T(8,128)(2,1)} %bitcast.76), custom_call_target="tpu_custom_call" | custom-call | tf_op jit(solution)/shard_map/tile_layer/pallas_call | solution.py:322
  73.4 1.0 convert_element_type.56
  74.8 86.8 %all-gather = bf16[128,768]{1,0:T(8,128)(2,1)S(1)} all-gather(bf16[16,768]{1,0:T(8,128)(2,1)S(1)} %convolution_convert_fusion), channel_id=2, replica_groups=mesh['seq'=16,'head'=8] {'head'}, dimensions={0}, use_global_device_ids=true | all-gather | bytes 221184 | tf_op jit(solution)/shard_map/all_gather | solution.py:425
  161.7 1.1 slice_select_fusion
  162.8 1.4 slice.22
  165.2 0.9 fusion.20
  166.2 0.8 copy.27
  167.1 1.2 reshape_reshape_squeeze.13
  168.3 0.8 copy.28
  169.1 2.0 reshape_reshape_squeeze.14
  171.1 0.9 copy.29
  171.9 2.0 reshape_reshape_squeeze.15
  174.1 4.4 %multiply_reduce_fusion.3 = (bf16[2,64,48]{2,0,1:T(2,128)(2,1)S(1)}, bf16[2,64,48]{2,0,1:T(2,128)(2,1)S(1)}, bf16[2,64,48]{2,0,1:T(2,128)(2,1)S(1)}) fusion(f32[2,16]{0,1:T(8,128)S(1)} %copy.57, bf16[64,16,2,48]{3,2,1,0:T(2,128)(2,1)S(1)} %reshape_reshape_squeeze.13, bf16[64,16,2,48]{3,2,1,0:T(2,128)(2,1)} %reshape_reshape_squeeze.14, ...), kind=kLoop, calls=%fused_computation.30 | loop fusion | flops 866304 | bytes 626816
  178.6 23.9 %all_gather.7 = bf16[1024,2,96]{2,1,0:T(2,128)(2,1)S(1)} all-gather(bf16[64,2,96]{2,1,0:T(2,128)(2,1)S(1)} %pad_maximum_fusion.3), channel_id=1, replica_groups=mesh['seq'=16,'head'=8] {'seq'}, dimensions={0}, use_global_device_ids=true | all-gather | bytes 417792 | tf_op jit(solution)/shard_map/all_gather | solution.py:455
  202.5 1.9 fusion.42
  204.5 1.5 fusion.43
  206.4 0.8 reshape_reshape_squeeze.12
  207.2 0.9 copy.25
  208.1 6.8 %while.2 = (s32[]{:T(128)}, f32[2,2,512]{2,1,0:T(2,128)S(1)}, f32[2,2,512]{2,1,0:T(2,128)S(1)}, f32[2,2,512,48]{2,3,1,0:T(8,128)}, bf16[2,512,2,48]{1,3,2,0:T(8,...) while((s32[]{:T(128)}, f32[2,2,512]{2,1,0:T(2,128)S(1)}, ...), condition=%wide.region_6.7_spmd, body=%wide.region_3.6_spmd.sunk | while | flops 209713152 | bytes 13304413 | solution.py:375
  208.2 0.8 multiply_reduce_fusion.5
  209.0 0.9 fusion.56
  209.9 1.6 fusion.57
  211.5 0.8 multiply_reduce_fusion.5
  212.4 0.9 fusion.56
  213.3 1.6 fusion.57
  215.2 1.8 copy.59
  217.0 1.3 fusion.25
  218.4 1.1 copy.33
  219.5 1.9 divide_convert_fusion
  (37 shorter events, 3.5 us)
Async XLA Ops:
  0.6 73.8 %copy-start = (bf16[1536,768]{1,0:T(8,128)(2,1)S(1)}, bf16[1536,768]{1,0:T(8,128)(2,1)}, u32[]{:S(2)}) copy-start(bf16[1536,768]{1,0:T(8,128)(2,1)} %param.17) | copy-start | bytes 7077892
  161.7 3.4 %copy-start.1 = (bf16[3,768,96]{1,2,0:T(8,128)(2,1)S(1)}, bf16[3,768,96]{1,2,0:T(8,128)(2,1)}, u32[]{:S(2)}) copy-start(bf16[3,768,96]{1,2,0:T(8,128)(2,1)} %param.20) | copy-start | bytes 1327108
  161.7 3.5 %copy-start.2 = (f32[768]{0:T(1024)S(1)}, f32[768]{0:T(1024)}, u32[]{:S(2)}) copy-start(f32[768]{0:T(1024)} %param.19) | copy-start | bytes 9220

commit v3 on v2

--- a/solution.py
+++ b/solution.py
@@ -351,50 +351,166 @@
     )(live, tiles, gain, weights)
 
 
-def partial_softmax(query_rows, key_rows, value_rows, score_scale):
-    rows = query_rows.shape[0]
-    block = min(512, rows)
-    grouped = query_rows.reshape(rows // block, block, query_rows.shape[1], query_rows.shape[2])
-
-    def one_block(block_rows):
-        scores = (
-            jnp.einsum("qhe,khe->hqk", block_rows, key_rows, preferred_element_type=jnp.float32)
-            * score_scale
+def slide_kernel(
+    emb_ref, proj_ref, cache_ref, gain_ref, w_ref, live_ref, out_ref,
+    fresh, far, qkv, near, fresh_send, fresh_recv, far_send, far_recv,
+):
+    seq, head = lax.axis_index("seq"), lax.axis_index("head")
+    groups, slots, width = fresh.shape
+    seqs = far.shape[0]
+    rows = cache_ref.shape[0]
+    span = groups * slots
+    heads = [(seq, (head + j) % groups) for j in range(1, groups)]
+    spots = [((seq + j) % seqs, head) for j in range(1, seqs)]
+    barrier = pltpu.get_barrier_semaphore()
+    for partner in heads + spots:
+        pl.semaphore_signal(barrier, inc=1, device_id=partner, device_id_type=MESH)
+
+    value = jnp.dot(
+        emb_ref[...].astype(jnp.bfloat16), proj_ref[...], preferred_element_type=jnp.float32
+    )
+    fresh[pl.ds(head, 1)] = value.astype(jnp.bfloat16)[None]
+    pl.semaphore_wait(barrier, len(heads) + len(spots))
+
+    def fresh_copy(j, slot):
+        return pltpu.make_async_remote_copy(
+            src_ref=fresh.at[slot],
+            dst_ref=fresh.at[slot],
+            send_sem=fresh_send.at[j],
+            recv_sem=fresh_recv.at[j],
+            device_id=heads[j],
+            device_id_type=MESH,
         )
-        highest = jnp.max(scores, axis=2)
-        weights = jnp.exp(scores - highest[:, :, None])
-        totals = jnp.sum(weights, axis=2)
-        numer = jnp.einsum(
-            "hqk,khe->hqe",
-            weights.astype(jnp.bfloat16),
-            value_rows,
-            preferred_element_type=jnp.float32,
+
+    def far_copy(j, slot):
+        return pltpu.make_async_remote_copy(
+            src_ref=far.at[slot],
+            dst_ref=far.at[slot],
+            send_sem=far_send.at[j],
+            recv_sem=far_recv.at[j],
+            device_id=spots[j],
+            device_id_type=MESH,
         )
-        return (highest, totals, numer)
-
-    highest, totals, numer = lax.map(one_block, grouped)
-    heads_here = query_rows.shape[1]
-    highest = jnp.transpose(highest, (1, 0, 2)).reshape(heads_here, rows)
-    totals = jnp.transpose(totals, (1, 0, 2)).reshape(heads_here, rows)
-    numer = jnp.transpose(numer, (1, 0, 2, 3)).reshape(heads_here, rows, query_rows.shape[2])
-    return (highest, totals, numer)
-
-
-def combine_levels(near, far, offsets):
-    near_top, near_total, near_numer = near
-    far_top, far_total, far_numer = far
-    rows = near_top.shape[1]
-    phase = jnp.arange(rows, dtype=jnp.int32) % RATE
-    picked = phase[None, :] == offsets[:, None]
-    far_top_rows = jnp.repeat(far_top, RATE, axis=1)
-    far_total_rows = jnp.repeat(far_total, RATE, axis=1)
-    far_numer_rows = jnp.repeat(far_numer, RATE, axis=1)
-    highest = jnp.where(picked, jnp.maximum(near_top, far_top_rows), near_top)
-    near_factor = jnp.exp(near_top - highest)
-    far_factor = jnp.where(picked, jnp.exp(jnp.minimum(far_top_rows - highest, 0.0)), 0.0)
-    numer = near_numer * near_factor[:, :, None] + far_numer_rows * far_factor[:, :, None]
-    totals = near_total * near_factor + far_total_rows * far_factor
-    return numer / totals[:, :, None]
+
+    for j in range(groups - 1):
+        fresh_copy(j, head).start()
+
+    def project(values):
+        normed = norm_rows(values, gain_ref[...]).astype(jnp.bfloat16)
+        return jnp.dot(normed, w_ref[...], preferred_element_type=jnp.float32).astype(jnp.bfloat16)
+
+    def cached(n, _):
+        at = pl.ds(pl.multiple_of(n * 128, 128), 128)
+        qkv[at, :] = project(cache_ref[at, :])
+        return 0
+
+    lax.fori_loop(span // 128, rows // 128, cached, 0)
+    for j in range(groups - 1):
+        fresh_copy(j, (head + groups - 1 - j) % groups).wait_recv()
+    mixed = jnp.where(
+        live_ref[...] > 0,
+        fresh[...].reshape(span, width).astype(jnp.float32),
+        cache_ref[0:span, :].astype(jnp.float32),
+    )
+    qkv[0:span, :] = project(mixed)
+
+    lane = lax.broadcasted_iota(jnp.int32, (1, 128), 1)
+    first = lane < SLIDE_HEAD_SIZE
+    thin = rows // RATE
+    pick_row = lax.broadcasted_iota(jnp.int32, (2 * thin, rows), 0)
+    pick_col = lax.broadcasted_iota(jnp.int32, (2 * thin, rows), 1)
+    offset = (2 * head + pick_row // thin) % RATE
+    pick = jnp.where(pick_col == (pick_row % thin) * RATE + offset, 1.0, 0.0).astype(jnp.bfloat16)
+    sparse = jnp.dot(pick, qkv[...], preferred_element_type=jnp.float32)
+    split = lax.broadcasted_iota(jnp.int32, (2 * thin, 128), 0) < thin
+    lanes2 = lax.broadcasted_iota(jnp.int32, (2 * thin, 128), 1)
+    own_lane = (lanes2 < SLIDE_HEAD_SIZE) == split
+    sparse_query = jnp.where(own_lane, sparse[:, :128], 0.0).astype(jnp.bfloat16)
+    pairs = []
+    for c in (1, 2):
+        values = sparse[:, c * 128 : (c + 1) * 128]
+        pairs.append(jnp.where(first, values[:thin], values[thin:]))
+    far[pl.ds(seq, 1)] = jnp.concatenate(pairs, axis=1).astype(jnp.bfloat16)[None]
+    for j in range(seqs - 1):
+        far_copy(j, seq).start()
+
+    scale = 1.0 / math.sqrt(SLIDE_HEAD_SIZE)
+    ones = jnp.ones((rows, 128), jnp.bfloat16)
+
+    def soften(scores):
+        top = jnp.max(scores, axis=1, keepdims=True)
+        return jnp.exp((scores - top) * scale).astype(jnp.bfloat16)
+
+    def near_block(n, _):
+        at = pl.ds(pl.multiple_of(n * 256, 256), 256)
+        parts = []
+        values = jnp.concatenate([qkv[:, 256:384], ones], axis=1)
+        for side in (first, jnp.logical_not(first)):
+            query = qkv[at, 0:128] * jnp.where(side, 1.0, 0.0).astype(jnp.bfloat16)
+            scores = lax.dot_general(
+                query, qkv[:, 128:256], (((1,), (1,)), ((), ())), preferred_element_type=jnp.float32
+            )
+            o = jnp.dot(soften(scores), values, preferred_element_type=jnp.float32)
+            parts.append(o[:, :128] / o[:, 128:])
+        near[at, :] = jnp.where(first, parts[0], parts[1])
+        return 0
+
+    lax.fori_loop(0, rows // 256, near_block, 0)
+
+    for j in range(seqs - 1):
+        far_copy(j, (seq + seqs - 1 - j) % seqs).wait_recv()
+    everyone = far[...].reshape(seqs * thin, 256)
+    keys = jnp.concatenate([qkv[:, 128:256], everyone[:, :128]], axis=0)
+    values = jnp.concatenate([qkv[:, 256:384], everyone[:, 128:]], axis=0)
+    values = jnp.concatenate([values, jnp.ones((rows + seqs * thin, 128), jnp.bfloat16)], axis=1)
+    scores = lax.dot_general(
+        sparse_query, keys, (((1,), (1,)), ((), ())), preferred_element_type=jnp.float32
+    )
+    o = jnp.dot(soften(scores), values, preferred_element_type=jnp.float32)
+    both = jnp.where(own_lane, o[:, :128] / o[:, 128:], 0.0).astype(jnp.bfloat16)
+    place_row = lax.broadcasted_iota(jnp.int32, (rows, 2 * thin), 0)
+    place_col = lax.broadcasted_iota(jnp.int32, (rows, 2 * thin), 1)
+    offset = (2 * head + place_col // thin) % RATE
+    place = jnp.where(place_row == (place_col % thin) * RATE + offset, 1.0, 0.0).astype(jnp.bfloat16)
+    spread = jnp.dot(place, both, preferred_element_type=jnp.float32)
+    row = lax.broadcasted_iota(jnp.int32, (rows, 128), 0)
+    side = lax.broadcasted_iota(jnp.int32, (rows, 128), 1) // SLIDE_HEAD_SIZE
+    picked = row % RATE == (2 * head + side) % RATE
+    result = jnp.where(picked, spread, near[...]).astype(jnp.bfloat16)
+    out_ref[...] = result[:, : out_ref.shape[1]]
+    for j in range(groups - 1):
+        fresh_copy(j, head).wait_send()
+    for j in range(seqs - 1):
+        far_copy(j, seq).wait_send()
+
+
+def encode_slide(embedded, proj, cache, gain, weights, live, groups, seqs):
+    slots, width = embedded.shape[0], proj.shape[1]
+    rows, columns = cache.shape[0], weights.shape[2]
+    padded = jnp.pad(weights, ((0, 0), (0, 0), (0, 128 - columns)))
+    padded = jnp.transpose(padded, (1, 0, 2)).reshape(width, 3 * 128)
+    dma = pltpu.SemaphoreType.DMA
+    vmem = pl.BlockSpec(memory_space=pltpu.VMEM)
+    return pl.pallas_call(
+        slide_kernel,
+        in_specs=[vmem] * 6,
+        out_specs=vmem,
+        out_shape=jax.ShapeDtypeStruct((rows, columns), jnp.bfloat16),
+        scratch_shapes=[
+            pltpu.VMEM((groups, slots, width), jnp.bfloat16),
+            pltpu.VMEM((seqs, rows // RATE, 256), jnp.bfloat16),
+            pltpu.VMEM((rows, 3 * 128), jnp.bfloat16),
+            pltpu.VMEM((rows, 128), jnp.float32),
+            dma((groups - 1,)),
+            dma((groups - 1,)),
+            dma((seqs - 1,)),
+            dma((seqs - 1,)),
+        ],
+        compiler_params=pltpu.CompilerParams(
+            collective_id=1, has_side_effects=True, vmem_limit_bytes=48 * 1024 * 1024
+        ),
+        name="slide_layer",
+    )(embedded, proj, cache, gain, padded, live)
 
 
 def per_device(
@@ -420,47 +536,11 @@
     live_count = jnp.sum(row_plan, axis=1)
     own_live = lax.dynamic_slice_in_dim(live_count, head_index, 1, 0)
     tile_layers, embedded = encode_tiles(own_live, local_tiles, tile_gain, weights)
-    slot_rows = embedded[:, 0].astype(jnp.bfloat16)
-    fresh = jnp.dot(slot_rows, slide_proj, preferred_element_type=jnp.float32).astype(jnp.bfloat16)
-    shared = lax.all_gather(fresh[None], "head", axis=0, tiled=True)
-    groups = shared.shape[0]
-    slide_width = shared.shape[2]
-    span = groups * slot_count
+    groups, seqs = send_map.shape[0], send_map.shape[1]
     places = jnp.arange(slot_count, dtype=jnp.int32)
-    live = (places[None, :] < live_count[:, None]).reshape(span)
-    head_part = jnp.where(live[:, None], shared.reshape(span, slide_width), slide_cache[:span])
-    slide_input = jnp.concatenate([head_part, slide_cache[span:]], axis=0)
-    seq_rows = slide_input.shape[0]
-    normed = norm_rows(slide_input, slide_gain).astype(jnp.bfloat16)
-    projected = jnp.einsum(
-        "tf,cfe->cte", normed, slide_qkv, preferred_element_type=jnp.float32
-    ).astype(jnp.bfloat16)
-    heads_here = slide_qkv.shape[2] // SLIDE_HEAD_SIZE
-    query_rows = projected[0].reshape(seq_rows, heads_here, SLIDE_HEAD_SIZE)
-    key_rows = projected[1].reshape(seq_rows, heads_here, SLIDE_HEAD_SIZE)
-    value_rows = projected[2].reshape(seq_rows, heads_here, SLIDE_HEAD_SIZE)
-    score_scale = 1.0 / math.sqrt(SLIDE_HEAD_SIZE)
-    near = partial_softmax(query_rows, key_rows, value_rows, score_scale)
-    offsets = (head_index * heads_here + jnp.arange(heads_here, dtype=jnp.int32)) % RATE
-    selector = (offsets[:, None] == jnp.arange(RATE, dtype=jnp.int32)[None, :]).astype(jnp.bfloat16)
-
-    def thin_rows(values):
-        grouped = values.reshape(seq_rows // RATE, RATE, heads_here, SLIDE_HEAD_SIZE)
-        return jnp.einsum(
-            "rphe,hp->rhe", grouped, selector, preferred_element_type=jnp.float32
-        ).astype(jnp.bfloat16)
-
-    sparse_query = thin_rows(query_rows)
-    both = jnp.concatenate([thin_rows(key_rows), thin_rows(value_rows)], axis=2)
-    both = lax.all_gather(both, "seq", axis=0, tiled=True)
-    far = partial_softmax(
-        sparse_query, both[:, :, :SLIDE_HEAD_SIZE], both[:, :, SLIDE_HEAD_SIZE:], score_scale
-    )
-    merged = combine_levels(near, far, offsets)
-    context = (
-        jnp.transpose(merged, (1, 0, 2))
-        .reshape(seq_rows, heads_here * SLIDE_HEAD_SIZE)
-        .astype(jnp.bfloat16)
+    live = (places[None, :] < live_count[:, None]).reshape(groups * slot_count, 1).astype(jnp.float32)
+    context = encode_slide(
+        embedded[:, 0], slide_proj, slide_cache, slide_gain[None], slide_qkv, live, groups, seqs
     )
     return (context, tile_layers[None, None])
 

time: 222 us -> 173 us (0.78)
  blocking collectives: 111 us -> 0 us
  Pallas kernels: 69.8 us -> 164 us
  other arithmetic: 13.8 us -> 1.28 us
  local copies, waits for them, and re-layouts: 17.1 us -> 7.05 us
  matrix products: 8.97 us -> 0 us
    all_gather x2 -> x0, blocking collectives: 111 us -> none  [the longest x1 86.8 us: per_device(): shared = lax.all_gather(fresh[None], 'head', axis=0, tiled=True)]
    pallas_call x1, Pallas kernels: 13 us -> 89.1 us  [encode_tiles(): pl.pallas_call(tile_kernel, grid_spec=pltpu.PrefetchScalarGridSpec(num_sc...]
    pallas_call x0 -> x1, Pallas kernels: none -> 17.9 us  [encode_slide(): pl.pallas_call(slide_kernel, in_specs=[vmem] * 6, out_specs=vmem, out_sha...]
    dot_general x7 -> x0, matrix products: 8.08 us -> none  [the longest x3 4.52 us: one_block(): jnp.einsum('hqk,khe->hqe', weights.astype(jnp.bfloat16), value_rows, pref...]
    another operation x4 -> x0, local copies, waits for them, and re-layouts: 6 us -> none  [the longest x3 5.19 us: thin_rows(): values.reshape(seq_rows // RATE, RATE, heads_here, SLIDE_HEAD_SIZE)]
    slice x6 -> x0, local copies, waits for them, and re-layouts: 5.85 us -> none  [the longest x1 1.85 us: per_device(): both[:, :, :SLIDE_HEAD_SIZE]]
    unnamed x2 -> x0, other arithmetic: 4.43 us -> none
    unnamed x7 -> x12, local copies, waits for them, and re-layouts: 0.11 us -> 3.97 us
where the time goes in v3:
time: 173 us
  Pallas kernels  164 us (95%)
  local copies, waits for them, and re-layouts  7.05 us (4%)
    pallas_call x1, Pallas kernels, encode_tiles(): pl.pallas_call(tile_kernel, grid_spec=pltpu.PrefetchScalarGridSpec(num_sc...  89.1 us
    pallas_call x1, Pallas kernels, gather_weights(): pl.pallas_call(gather_kernel, in_specs=[pl.BlockSpec(memory_space=pltpu.V...  56.8 us
    pallas_call x1, Pallas kernels, encode_slide(): pl.pallas_call(slide_kernel, in_specs=[vmem] * 6, out_specs=vmem, out_sha...  17.9 us
    unnamed x12, local copies, waits for them, and re-layouts  3.97 us

profile of v3, /device:TPU:0, one launch (start us, length us, event | category | flops | bytes accessed | tf_op | source)
XLA Modules:
  0.0 172.9 jit_solution(14822132984128128190)
XLA Ops:
  0.6 0.0 copy-start
  0.6 0.8 copy-done
  1.5 0.2 dynamic-slice_reduce_fusion
  1.7 0.6 dynamic_slice.8.live_ref
  2.3 1.0 pad_maximum_fusion
  3.3 0.1 reshape.45
  3.4 0.1 copy.16
  3.5 56.8 %weight_gather.1 = bf16[4,2,2,3,4,4,2,48,128]{8,7,6,5,4,3,2,1,0:T(8,128)(2,1)} custom-call(bf16[4,48,384]{2,1,0:T(8,128)(2,1)S(1)} %copy.17.w_ref), custom_call_target="tpu_custom_call" | custom-call | tf_op jit(solution)/shard_map/weight_gather/pallas_call | solution.py:192
  60.3 0.0 copy-start.3
  60.3 0.0 copy-start.4
  60.3 0.0 copy-start.1
  60.3 89.1 %tile_layer.1 = (bf16[16,128,1536]{2,1,0:T(8,128)(2,1)}, f32[16,1,1536]{2,1,0:T(1,128)}) custom-call(s32[1]{0:T(128)} %dynamic_slice.8.live_ref, bf16[16,128,1536]{2,1,0:T(8,128)(2,1)} %bitcast.14, f32[2,1536]{1,0:T(2,128)} %gain_ref.1, bf16[4,12,1536,128]{3,2,1,0:T(8,128)(2,1)} %bitcast.13), custom_call_target="tpu_custom_call" | custom-call | tf_op jit(solution)/shard_map/tile_layer/pallas_call | solution.py:322
  149.4 0.9 copy.23
  150.3 0.1 fusion
  150.4 0.1 reshape.50.live_ref
  150.5 0.0 copy-done.3
  150.5 0.9 pad.4
  151.3 1.4 copy.18.w_ref
  152.7 0.0 copy-done.4
  152.7 0.0 copy-done.1
  152.7 0.0 copy-start.2
  152.8 1.4 copy-done.2
  154.2 17.9 %slide_layer.1 = bf16[1024,96]{1,0:T(8,128)(2,1)S(1)} custom-call(f32[16,1536]{1,0:T(8,128)S(1)} %bitcast.12, bf16[1536,768]{1,0:T(8,128)(2,1)S(1)} %copy-done.1, bf16[1024,768]{1,0:T(8,128)(2,1)S(1)} %copy-done.2, f32[1,768]{1,0:T(1,128)S(1)} %broadcast_in_dim.8.gain_ref, bf16[768,384]{1,0:T(8,128)(2,1)S(1)} %copy.18.w_ref, f32[128,1]{1,0:T(8,128)S(1)} %reshape.50.live_ref), custom_call_target="tpu_custom_call" | custom-call | tf_op jit(solution)/shard_map/slide_layer/pallas_call | solution.py:494
  172.1 0.8 copy.20
  (2 shorter events, 0.0 us)
Async XLA Ops:
  0.6 0.8 copy-start
  60.3 90.2 %copy-start.3 = (bf16[3,768,96]{1,2,0:T(8,128)(2,1)S(1)}, bf16[3,768,96]{1,2,0:T(8,128)(2,1)}, u32[]{:S(2)}) copy-start(bf16[3,768,96]{1,2,0:T(8,128)(2,1)} %param.18) | copy-start | bytes 1327108
  60.3 92.4 %copy-start.4 = (f32[768]{0:T(1024)S(1)}, f32[768]{0:T(1024)}, u32[]{:S(2)}) copy-start(f32[768]{0:T(1024)} %param.17) | copy-start | bytes 9220
  60.3 92.4 %copy-start.1 = (bf16[1536,768]{1,0:T(8,128)(2,1)S(1)}, bf16[1536,768]{1,0:T(8,128)(2,1)}, u32[]{:S(2)}) copy-start(bf16[1536,768]{1,0:T(8,128)(2,1)} %proj_ref.1) | copy-start | bytes 7077892
  152.7 1.4 copy-start.2

commit v4 on v3

--- a/solution.py
+++ b/solution.py
@@ -11,11 +11,19 @@
 SLIDE_HEAD_SIZE = 48
 RATE = 16
 EPS = 1e-05
-GROUP = 4
+GROUP = 2
 COLS = 512
 MESH = pl.DeviceIdType.MESH
 ORDERS = (("x", "y", "z"), ("y", "z", "x"), ("z", "x", "y"))
 RING = 4
+ROWS = 512
+
+
+def norm_rows(values, gain):
+    values = values.astype(jnp.float32)
+    center = values - jnp.mean(values, axis=-1, keepdims=True)
+    spread = jnp.mean(center * center, axis=-1, keepdims=True)
+    return center * lax.rsqrt(spread + EPS) * gain
 
 
 class Place:
@@ -55,8 +63,56 @@
         )
 
 
-def gather_kernel(w_ref, full, inbox, own, swap_send, swap_recv, send, recv, pair_send, pair_recv, keep):
+def gather_kernel(
+    w_ref, x_ref, gain_ref, kvq_ref, last_ref, full, rows_ref, stage, inbox, own,
+    swap_send, swap_recv, send, recv, pair_send, pair_recv, keep, store, load,
+):
     here = Place()
+    length = rows_ref.shape[0]
+    load_copy = pltpu.make_async_copy(x_ref, rows_ref, load)
+    load_copy.start()
+
+    def normalise(start, count):
+        def step(r, _):
+            at = pl.ds(pl.multiple_of(r * 32, 32), 32)
+            rows_ref[at, :] = norm_rows(rows_ref[at, :], gain_ref[0:1, :]).astype(jnp.bfloat16)
+            return 0
+
+        lax.fori_loop(start, start + count, step, 0)
+
+    def ref_of(spots):
+        m = spots[0]
+        return full.at[spots] if m < 3 else last_ref.at[spots[1:]]
+
+    def store_copy(m, slot, low, block):
+        return pltpu.make_async_copy(
+            stage.at[slot],
+            kvq_ref.at[m, pl.ds(low * 6, 6), pl.ds(pl.multiple_of(block * ROWS, ROWS), ROWS), :],
+            store.at[slot],
+        )
+
+    blocks = length // ROWS
+
+    def multiply(m, start, count):
+        def step(u, _):
+            slot, low, block = u % 2, u // blocks, u % blocks
+
+            @pl.when(m * 2 * blocks + u >= 2)
+            def _():
+                store_copy(m, slot, low, block).wait()
+
+            at = pl.ds(pl.multiple_of(block * ROWS, ROWS), ROWS)
+            width = rows_ref.shape[1]
+            w = jnp.concatenate(
+                [full[m, low, j // 3, j % 3].reshape(width, 128) for j in range(6)], axis=1
+            )
+            y = jnp.dot(rows_ref[at, :], w, preferred_element_type=jnp.float32).astype(jnp.bfloat16)
+            for j in range(6):
+                stage[slot, j] = y[:, j * 128 : (j + 1) * 128]
+            store_copy(m, slot, low, block).start()
+            return 0
+
+        lax.fori_loop(start, start + count, step, 0)
     core, other = here.core, 1 - here.core
     x = here.at["x"]
     low = x % 2
@@ -85,6 +141,9 @@
             )
         )
         swaps[n].start()
+    load_copy.wait()
+    share = -(-length // 32 // 6)
+    normalise(0, share)
     for n in range(3):
         swaps[n].wait_recv()
     count = 4 * 48
@@ -106,10 +165,10 @@
     def move(m, p, phase, piece, origin, target):
         spots = here.index(m, core, p, phase, origin)
         axis = ORDERS[p][phase]
-        src = own.at[m, p] if phase == 0 and origin == 0 else full.at[spots]
+        src = own.at[m, p] if phase == 0 and origin == 0 else ref_of(spots)
         return pltpu.make_async_remote_copy(
             src_ref=src,
-            dst_ref=full.at[spots],
+            dst_ref=ref_of(spots),
             send_sem=send.at[m, p, phase, piece],
             recv_sem=recv.at[m, p, phase, piece],
             device_id=here.device(axis, target),
@@ -120,8 +179,8 @@
         spots = here.index(m, core, p, phase, origin)
         axis = ORDERS[p][phase]
         pltpu.make_async_remote_copy(
-            src_ref=full.at[spots],
-            dst_ref=full.at[spots],
+            src_ref=ref_of(spots),
+            dst_ref=ref_of(spots),
             send_sem=send.at[m, p, phase, piece],
             recv_sem=recv.at[m, p, phase, piece],
             device_id=here.device(axis, 1),
@@ -131,8 +190,8 @@
     def pair(m, p, piece, phase, origin, side):
         spots = here.index(m, side, p, phase, origin)
         return pltpu.make_async_remote_copy(
-            src_ref=full.at[spots],
-            dst_ref=full.at[spots],
+            src_ref=ref_of(spots),
+            dst_ref=ref_of(spots),
             send_sem=pair_send.at[m, p, piece],
             recv_sem=pair_recv.at[m, p, piece],
             device_id=members[0],
@@ -151,52 +210,109 @@
         go(move(m, p, 0, 0, 0, 1))
         go(move(m, p, 0, 1, 0, 3))
     for m, p in todo:
-        copy = pltpu.make_async_copy(own.at[m, p], full.at[here.index(m, core, p, 0, 0)], keep.at[m, p])
+        copy = pltpu.make_async_copy(own.at[m, p], ref_of(here.index(m, core, p, 0, 0)), keep.at[m, p])
         copy.start()
         keeps.append(copy)
     for copy in keeps:
         copy.wait()
-    for phase in range(3):
-        for m, p in todo:
-            arrive(m, p, phase, 0, 3)
-            arrive(m, p, phase, 1, 1)
-            if m % 2 == 0:
-                go(move(m, p, phase, 2, 3, 1))
-            else:
-                go(move(m, p, phase, 2, 1, 3))
-            if phase == 2:
-                go(pair(m, p, 1, 2, 3, core))
-                go(pair(m, p, 2, 2, 1, core))
-        for m, p in todo:
-            arrive(m, p, phase, 2, 2)
-            if phase < 2:
-                go(move(m, p, phase + 1, 0, 0, 1))
-                go(move(m, p, phase + 1, 1, 0, 3))
-            if phase == 1:
-                go(pair(m, p, 0, 2, 0, core))
-            if phase == 2:
-                go(pair(m, p, 3, 2, 2, core))
-    for m, p in todo:
+    done = [share]
+
+    def norm_some():
+        count = min(share, length // 32 - done[0])
+        normalise(done[0], count)
+        done[0] += count
+
+    def first_arrivals(m, p, phase):
+        arrive(m, p, phase, 0, 3)
+        arrive(m, p, phase, 1, 1)
+        if m % 2 == 0:
+            go(move(m, p, phase, 2, 3, 1))
+        else:
+            go(move(m, p, phase, 2, 1, 3))
+        if phase == 2:
+            go(pair(m, p, 1, 2, 3, core))
+            go(pair(m, p, 2, 2, 1, core))
+
+    def start_phase(m, p, phase):
+        go(move(m, p, phase, 0, 0, 1))
+        go(move(m, p, phase, 1, 0, 3))
+
+    def last_arrival(m, p, phase):
+        arrive(m, p, phase, 2, 2)
+        if phase == 0 or (phase == 1 and m < 2):
+            start_phase(m, p, phase + 1)
+        if phase == 1:
+            go(pair(m, p, 0, 2, 0, core))
+        if phase == 2:
+            go(pair(m, p, 3, 2, 2, core))
+
+    def from_pair(m, p):
         for piece, origin in enumerate((0, 3, 1, 2)):
             pair(m, p, piece, 2, origin, other).wait_recv()
+
+    def every(step, m, *rest):
+        for p in range(3):
+            step(m, p, *rest)
+
+    norm_some()
+    for phase in range(2):
+        for m in range(4):
+            every(first_arrivals, m, phase)
+        norm_some()
+        for m in range(4):
+            every(last_arrival, m, phase)
+        norm_some()
+    every(first_arrivals, 0, 2)
+    every(start_phase, 2, 2)
+    every(last_arrival, 0, 2)
+    every(first_arrivals, 1, 2)
+    every(start_phase, 3, 2)
+    every(from_pair, 0)
+    multiply(0, 0, blocks)
+    every(last_arrival, 1, 2)
+    multiply(0, blocks, blocks)
+    every(first_arrivals, 2, 2)
+    every(from_pair, 1)
+    multiply(1, 0, blocks)
+    every(last_arrival, 2, 2)
+    multiply(1, blocks, blocks)
+    every(first_arrivals, 3, 2)
+    every(from_pair, 2)
+    multiply(2, 0, blocks)
+    every(last_arrival, 3, 2)
+    multiply(2, blocks, blocks)
+    every(from_pair, 3)
+    for slot in range(2):
+        store_copy(2, slot, 1, blocks - 2 + slot).wait()
     for copy in swaps + sent:
         copy.wait_send()
 
 
-def gather_weights(wq, wkv, wo):
+def project_tiles(tiles, gain, wq, wkv, wo):
     rows, width = wq.shape
+    slots, length, _ = tiles.shape
+    count = slots * length
     parts = jnp.concatenate([wkv, wq, wo], axis=1)
     parts = parts.reshape(rows, 4, 4, width // 4)
     parts = jnp.transpose(parts, (2, 1, 0, 3)).reshape(4, 4 * rows, width // 4)
     dma = pltpu.SemaphoreType.DMA
+    hbm = pl.BlockSpec(memory_space=pl.ANY)
+    vmem = pl.BlockSpec(memory_space=pltpu.VMEM)
+    one = (2, 2, 3, 4, 4, 2, 4 * rows, 128)
     return pl.pallas_call(
         gather_kernel,
-        in_specs=[pl.BlockSpec(memory_space=pltpu.VMEM)],
-        out_specs=pl.BlockSpec(memory_space=pl.ANY),
-        out_shape=jax.ShapeDtypeStruct((4, 2, 2, 3, 4, 4, 2, 48, 128), jnp.bfloat16),
+        in_specs=[vmem, hbm, vmem],
+        out_specs=[hbm, hbm],
+        out_shape=[
+            jax.ShapeDtypeStruct((3, width // 128, count, 128), jnp.bfloat16),
+            jax.ShapeDtypeStruct(one, jnp.bfloat16),
+        ],
         scratch_shapes=[
-            pltpu.VMEM((3, 48, 384), jnp.bfloat16),
-            pltpu.VMEM((4, 3, 48, 128), jnp.bfloat16),
+            pltpu.VMEM((3,) + one, jnp.bfloat16),
+            pltpu.VMEM((count, width), jnp.bfloat16),
+            pltpu.VMEM((2, 6, ROWS, 128), jnp.bfloat16),
+            pltpu.VMEM((3, 4 * rows, width // 4), jnp.bfloat16),
+            pltpu.VMEM((4, 3, 4 * rows, 128), jnp.bfloat16),
             dma((3,)),
             dma((3,)),
             dma((4, 3, 3, 3)),
@@ -204,76 +320,39 @@
             dma((4, 3, 4)),
             dma((4, 3, 4)),
             dma((4, 3)),
+            dma((2,)),
+            dma,
         ],
-        compiler_params=pltpu.CompilerParams(collective_id=0, has_side_effects=True, vmem_limit_bytes=40 * 1024 * 1024),
-        name="weight_gather",
-    )(parts)
-
-
-def norm_rows(values, gain):
-    values = values.astype(jnp.float32)
-    center = values - jnp.mean(values, axis=-1, keepdims=True)
-    spread = jnp.mean(center * center, axis=-1, keepdims=True)
-    return center * lax.rsqrt(spread + EPS) * gain
-
-
-def tile_kernel(live_ref, x_ref, gain_ref, w_ref, out_ref, emb_ref, w, xn, q, kv, ctx, load):
+        compiler_params=pltpu.CompilerParams(
+            collective_id=0, has_side_effects=True, vmem_limit_bytes=48 * 1024 * 1024
+        ),
+        name="gather_project",
+    )(parts, tiles.reshape(count, width), gain)
+
+
+def tile_kernel(live_ref, x_ref, gain_ref, kvq, wo_ref, out_ref, emb_ref, wo, ctx, load):
     step = pl.program_id(0)
     live = live_ref[0]
     tiles, length, width = x_ref.shape
-    blocks = COLS // 128
-    loads = [pltpu.make_async_copy(w_ref.at[m], w.at[m], load.at[m]) for m in range(4)]
+    pairs = width // 128
+    load_copy = pltpu.make_async_copy(wo_ref, wo, load)
 
     @pl.when(step == 0)
     def _():
-        for copy in loads:
-            copy.start()
-
-    def ready(m):
-        @pl.when(step == 0)
-        def _():
-            loads[m].wait()
-
-    def columns(m, n):
-        return jnp.concatenate([w[m, n * blocks + j] for j in range(blocks)], axis=1)
+        load_copy.start()
 
     @pl.when(step * tiles < live)
     def _():
-        for t in range(tiles):
-
-            def norm(r, _):
-                at = pl.ds(pl.multiple_of(r * 32, 32), 32)
-                values = norm_rows(x_ref[t, at, :], gain_ref[0:1, :])
-                xn[pl.ds(pl.multiple_of(t * length + r * 32, 32), 32), :] = values.astype(jnp.bfloat16)
-                return 0
-
-            lax.fori_loop(0, length // 32, norm, 0)
-
-        for m, ref, base in ((0, kv, 0), (1, kv, width), (2, q, 0)):
-            ready(m)
-
-            def project(n, _):
-                at = pl.ds(pl.multiple_of(base + n * COLS, COLS), COLS)
-                ref[:, at] = jnp.dot(
-                    xn[...], columns(m, n), preferred_element_type=jnp.float32
-                ).astype(jnp.bfloat16)
-                return 0
-
-            lax.fori_loop(0, width // COLS, project, 0)
-
         lane = lax.broadcasted_iota(jnp.int32, (length, 128), 1)
         first = lane < TILE_HEAD_SIZE
         ones_a = jnp.where(first, 1.0, 0.0).astype(jnp.bfloat16)
         ones_b = jnp.where(first, 0.0, 1.0).astype(jnp.bfloat16)
         ones = jnp.concatenate([ones_a, ones_b], axis=0)
-        scale = 1.0 / math.sqrt(TILE_HEAD_SIZE)
-
-        def attend(p, _):
-            at = pl.ds(pl.multiple_of(p * 128, 128), 128)
-            vat = pl.ds(pl.multiple_of(width + p * 128, 128), 128)
+        scale = math.log2(math.e) / math.sqrt(TILE_HEAD_SIZE)
+        for p in range(pairs):
             for t in range(tiles):
-                tat = slice(t * length, (t + 1) * length)
-                qp, kp, vp = q[tat, at], kv[tat, at], kv[tat, vat]
+                at = slice(t * length, (t + 1) * length)
+                kp, vp, qp = kvq[0, p, at, :], kvq[1, p, at, :], kvq[2, p, at, :]
                 keys = jnp.concatenate([kp * ones_a, kp * ones_b], axis=0)
                 vals = jnp.concatenate([vp * ones_a, vp * ones_b], axis=0)
                 vals = jnp.concatenate([vals, ones], axis=1)
@@ -284,19 +363,24 @@
                 for half in range(2):
                     sh = s[:, half * length : (half + 1) * length]
                     top = jnp.max(sh, axis=1, keepdims=True)
-                    parts.append(jnp.exp((sh - top) * scale).astype(jnp.bfloat16))
-                w = jnp.concatenate(parts, axis=1)
-                o = jnp.dot(w, vals, preferred_element_type=jnp.float32)
-                ctx[tat, at] = (o[:, :128] / o[:, 128:]).astype(jnp.bfloat16)
-            return 0
-
-        lax.fori_loop(0, width // 128, attend, 0)
-
-        ready(3)
-
+                    parts.append(jnp.exp2((sh - top) * scale).astype(jnp.bfloat16))
+                o = jnp.dot(
+                    jnp.concatenate(parts, axis=1), vals, preferred_element_type=jnp.float32
+                )
+                ctx[p, at, :] = (o[:, :128] / o[:, 128:]).astype(jnp.bfloat16)
+
+    @pl.when(step == 0)
+    def _():
+        load_copy.wait()
+
+    @pl.when(step * tiles < live)
+    def _():
         def project_out(n, _):
             at = pl.ds(pl.multiple_of(n * COLS, COLS), COLS)
-            y = jnp.dot(ctx[...], columns(3, n), preferred_element_type=jnp.float32)
+            blocks = COLS // 128
+            context = jnp.concatenate([ctx[j] for j in range(pairs)], axis=1)
+            w = jnp.concatenate([wo[n * blocks + j] for j in range(blocks)], axis=1)
+            y = jnp.dot(context, w, preferred_element_type=jnp.float32)
             for t in range(tiles):
                 xt = x_ref[t, :, at].astype(jnp.float32)
                 yt = xt + y[t * length : (t + 1) * length]
@@ -309,16 +393,13 @@
 
     @pl.when(step * tiles >= live)
     def _():
-        for m in range(4):
-            ready(m)
         out_ref[...] = jnp.zeros_like(out_ref)
         emb_ref[...] = jnp.zeros_like(emb_ref)
 
 
-def encode_tiles(live, tiles, gain, weights):
+def encode_tiles(live, tiles, gain, kvq, wo):
     slots, length, width = tiles.shape
     rows = GROUP * length
-    whole = pl.BlockSpec(memory_space=pltpu.VMEM)
     return pl.pallas_call(
         tile_kernel,
         grid_spec=pltpu.PrefetchScalarGridSpec(
@@ -326,7 +407,8 @@
             grid=(slots // GROUP,),
             in_specs=[
                 pl.BlockSpec((GROUP, length, width), lambda i, live: (i, 0, 0)),
-                whole,
+                pl.BlockSpec(memory_space=pltpu.VMEM),
+                pl.BlockSpec((3, width // 128, rows, 128), lambda i, live: (0, 0, i, 0)),
                 pl.BlockSpec(memory_space=pl.ANY),
             ],
             out_specs=[
@@ -334,21 +416,18 @@
                 pl.BlockSpec((GROUP, 1, width), lambda i, live: (i, 0, 0)),
             ],
             scratch_shapes=[
-                pltpu.VMEM((4, width // 128, width, 128), jnp.bfloat16),
-                pltpu.VMEM((rows, width), jnp.bfloat16),
-                pltpu.VMEM((rows, width), jnp.bfloat16),
-                pltpu.VMEM((rows, 2 * width), jnp.bfloat16),
-                pltpu.VMEM((rows, width), jnp.bfloat16),
-                pltpu.SemaphoreType.DMA((4,)),
+                pltpu.VMEM((width // 128, width, 128), jnp.bfloat16),
+                pltpu.VMEM((width // 128, rows, 128), jnp.bfloat16),
+                pltpu.SemaphoreType.DMA,
             ],
         ),
         out_shape=[
             jax.ShapeDtypeStruct((slots, length, width), jnp.bfloat16),
             jax.ShapeDtypeStruct((slots, 1, width), jnp.float32),
         ],
-        compiler_params=pltpu.CompilerParams(vmem_limit_bytes=56 * 1024 * 1024),
+        compiler_params=pltpu.CompilerParams(vmem_limit_bytes=48 * 1024 * 1024),
         name="tile_layer",
-    )(live, tiles, gain, weights)
+    )(live, tiles, gain, kvq, wo)
 
 
 def slide_kernel(
@@ -529,13 +608,12 @@
     slot_count = local_tiles.shape[0]
     seq_index = lax.axis_index("seq")
     head_index = lax.axis_index("head")
-    weights = gather_weights(tile_wq, tile_wkv, tile_wo)
-    width = local_tiles.shape[2]
-    weights = weights.reshape(4, width // 128, width, 128)
+    kvq, w_out = project_tiles(local_tiles, tile_gain, tile_wq, tile_wkv, tile_wo)
+    w_out = w_out.reshape(kvq.shape[1], -1, 128)
     row_plan = lax.dynamic_index_in_dim(send_map, seq_index, 1, keepdims=False)
     live_count = jnp.sum(row_plan, axis=1)
     own_live = lax.dynamic_slice_in_dim(live_count, head_index, 1, 0)
-    tile_layers, embedded = encode_tiles(own_live, local_tiles, tile_gain, weights)
+    tile_layers, embedded = encode_tiles(own_live, local_tiles, tile_gain, kvq, w_out)
     groups, seqs = send_map.shape[0], send_map.shape[1]
     places = jnp.arange(slot_count, dtype=jnp.int32)
     live = (places[None, :] < live_count[:, None]).reshape(groups * slot_count, 1).astype(jnp.float32)

time: 173 us -> 139 us (0.80)
  Pallas kernels: 164 us -> 130 us
    pallas_call x1, Pallas kernels: 89.1 us -> 12.9 us  [encode_tiles(): pl.pallas_call(tile_kernel, grid_spec=pltpu.PrefetchScalarGridSpec(num_sc...]
    pallas_call x1, Pallas kernels: 56.8 us -> 81.2 us  [project_tiles(): pl.pallas_call(gather_kernel, in_specs=[vmem, hbm, vmem], out_specs=[hbm,...]
    pallas_call x1, Pallas kernels: 17.9 us -> 35.8 us  [encode_slide(): pl.pallas_call(slide_kernel, in_specs=[vmem] * 6, out_specs=vmem, out_sha...]
    unnamed x12 -> x14, local copies, waits for them, and re-layouts: 3.97 us -> 3.78 us
where the time goes in v4:
time: 139 us
  Pallas kernels  130 us (94%)
  local copies, waits for them, and re-layouts  6.85 us (5%)
    pallas_call x1, Pallas kernels, project_tiles(): pl.pallas_call(gather_kernel, in_specs=[vmem, hbm, vmem], out_specs=[hbm,...  81.2 us
    pallas_call x1, Pallas kernels, encode_slide(): pl.pallas_call(slide_kernel, in_specs=[vmem] * 6, out_specs=vmem, out_sha...  35.8 us
    pallas_call x1, Pallas kernels, encode_tiles(): pl.pallas_call(tile_kernel, grid_spec=pltpu.PrefetchScalarGridSpec(num_sc...  12.9 us
    unnamed x14, local copies, waits for them, and re-layouts  3.78 us

profile of v4, /device:TPU:0, one launch (start us, length us, event | category | flops | bytes accessed | tf_op | source)
XLA Modules:
  0.0 138.8 jit_solution(11073296272247060449)
XLA Ops:
  0.6 0.0 copy-start
  0.6 0.8 copy-done
  1.5 0.2 dynamic-slice_reduce_fusion
  1.7 0.6 dynamic_slice.8.live_ref
  2.3 1.0 pad_maximum_fusion
  3.3 0.1 reshape.45
  3.4 0.1 copy.16
  3.5 0.0 copy-start.3
  3.5 0.7 copy-done.3
  4.2 81.2 %gather_project.1 = (bf16[3,12,2048,128]{3,2,1,0:T(8,128)(2,1)}, bf16[2,2,3,4,4,2,48,128]{7,6,5,4,3,2,1,0:T(8,128)(2,1)S(1)}) custom-call(bf16[4,48,384]{2,1,0:T(8,128)(2,1)S(1)} %copy.17.w_ref, bf16[2048,1536]{1,0:T(8,128)(2,1)} %bitcast.15, f32[2,1536]{1,0:T(2,128)S(1)} %copy-done.3), custom_call_target="tpu_custom_call" | custom-call | tf_op jit(solution)/shard_map/gather_project/pallas_call | solution.py:302
  85.3 0.0 copy-start.4
  85.3 0.0 copy-start.5
  85.4 0.0 copy-start.1
  85.4 12.9 %tile_layer.1 = (bf16[16,128,1536]{2,1,0:T(8,128)(2,1)}, f32[16,1,1536]{2,1,0:T(1,128)S(1)}) custom-call(s32[1]{0:T(128)} %dynamic_slice.8.live_ref, bf16[16,128,1536]{2,1,0:T(8,128)(2,1)} %bitcast.16, f32[2,1536]{1,0:T(2,128)S(1)} %copy-done.3, bf16[3,12,2048,128]{3,2,1,0:T(8,128)(2,1)} %get-tuple-element.6.kvq, bf16[12,1536,128]{2,1,0:T(8,128)(2,1)S(1)} %bitcast.13), custom_call_target="tpu_custom_call" | custom-call | tf_op jit(solution)/shard_map/tile_layer/pallas_call | solution.py:403
  98.3 0.1 fusion
  98.4 0.1 reshape.50.live_ref
  98.5 0.0 copy-done.4
  98.5 0.9 pad.4
  99.4 1.4 copy.18.w_ref
  100.7 0.0 copy-done.5
  100.8 0.0 copy-done.1
  100.8 0.0 copy-start.2
  100.8 1.4 %copy-done.2 = bf16[1024,768]{1,0:T(8,128)(2,1)S(1)} copy-done((bf16[1024,768]{1,0:T(8,128)(2,1)S(1)}, bf16[1024,768]{1,0:T(8,128)(2,1)}, u32[]{:S(2)}) %copy-start.2) | copy-done | bytes 1572888
  102.2 35.8 %slide_layer.1 = bf16[1024,96]{1,0:T(8,128)(2,1)S(1)} custom-call(f32[16,1536]{1,0:T(8,128)S(1)} %bitcast.14, bf16[1536,768]{1,0:T(8,128)(2,1)S(1)} %copy-done.1, bf16[1024,768]{1,0:T(8,128)(2,1)S(1)} %copy-done.2, f32[1,768]{1,0:T(1,128)S(1)} %broadcast_in_dim.8.gain_ref, bf16[768,384]{1,0:T(8,128)(2,1)S(1)} %copy.18.w_ref, f32[128,1]{1,0:T(8,128)S(1)} %reshape.50.live_ref), custom_call_target="tpu_custom_call" | custom-call | tf_op jit(solution)/shard_map/slide_layer/pallas_call | solution.py:573
  138.0 0.8 copy.20
  (3 shorter events, 0.0 us)
Async XLA Ops:
  0.6 0.8 copy-start
  3.5 0.7 copy-start.3
  85.3 13.2 %copy-start.4 = (bf16[3,768,96]{1,2,0:T(8,128)(2,1)S(1)}, bf16[3,768,96]{1,2,0:T(8,128)(2,1)}, u32[]{:S(2)}) copy-start(bf16[3,768,96]{1,2,0:T(8,128)(2,1)} %param.18) | copy-start | bytes 1327108
  85.3 15.4 %copy-start.5 = (f32[768]{0:T(1024)S(1)}, f32[768]{0:T(1024)}, u32[]{:S(2)}) copy-start(f32[768]{0:T(1024)} %param.17) | copy-start | bytes 9220
  85.4 15.4 %copy-start.1 = (bf16[1536,768]{1,0:T(8,128)(2,1)S(1)}, bf16[1536,768]{1,0:T(8,128)(2,1)}, u32[]{:S(2)}) copy-start(bf16[1536,768]{1,0:T(8,128)(2,1)} %proj_ref.1) | copy-start | bytes 7077892
  100.8 1.4 %copy-start.2 = (bf16[1024,768]{1,0:T(8,128)(2,1)S(1)}, bf16[1024,768]{1,0:T(8,128)(2,1)}, u32[]{:S(2)}) copy-start(bf16[1024,768]{1,0:T(8,128)(2,1)} %cache_ref.1) | copy-start | bytes 4718596

commit v5 on v4

--- a/solution.py
+++ b/solution.py
@@ -24,6 +24,15 @@
     center = values - jnp.mean(values, axis=-1, keepdims=True)
     spread = jnp.mean(center * center, axis=-1, keepdims=True)
     return center * lax.rsqrt(spread + EPS) * gain
+
+
+def project_slide(values, gain, w_ref):
+    normed = norm_rows(values, gain).astype(jnp.bfloat16)
+    parts = []
+    for c in range(3):
+        y = jnp.dot(normed, w_ref[c], preferred_element_type=jnp.float32)
+        parts += [y, jnp.zeros((y.shape[0], 128 - y.shape[1]), jnp.float32)]
+    return jnp.concatenate(parts, axis=1).astype(jnp.bfloat16)
 
 
 class Place:
@@ -64,8 +73,9 @@
 
 
 def gather_kernel(
-    w_ref, x_ref, gain_ref, kvq_ref, last_ref, full, rows_ref, stage, inbox, own,
-    swap_send, swap_recv, send, recv, pair_send, pair_recv, keep, store, load,
+    w_ref, x_ref, gain_ref, cache_ref, slide_gain_ref, slide_w_ref,
+    kvq_ref, last_ref, slide_ref, full, rows_ref, stage, inbox, own, slide_rows,
+    swap_send, swap_recv, send, recv, pair_send, pair_recv, keep, store, load, slide_store,
 ):
     here = Place()
     length = rows_ref.shape[0]
@@ -222,6 +232,17 @@
         normalise(done[0], count)
         done[0] += count
 
+    def slide_some(start, count):
+        def step(n, _):
+            at = pl.ds(pl.multiple_of(n * 128, 128), 128)
+            slide_rows[at, :] = project_slide(cache_ref[at, :], slide_gain_ref[...], slide_w_ref)
+            return 0
+
+        lax.fori_loop(start, start + count, step, 0)
+
+    slide_copy = pltpu.make_async_copy(slide_rows, slide_ref, slide_store)
+    quarter = cache_ref.shape[0] // 128 // 4
+
     def first_arrivals(m, p, phase):
         arrive(m, p, phase, 0, 3)
         arrive(m, p, phase, 1, 1)
@@ -259,9 +280,12 @@
         for m in range(4):
             every(first_arrivals, m, phase)
         norm_some()
+        slide_some(2 * phase * quarter, quarter)
         for m in range(4):
             every(last_arrival, m, phase)
         norm_some()
+        slide_some((2 * phase + 1) * quarter, quarter)
+    slide_copy.start()
     every(first_arrivals, 0, 2)
     every(start_phase, 2, 2)
     every(last_arrival, 0, 2)
@@ -284,11 +308,12 @@
     every(from_pair, 3)
     for slot in range(2):
         store_copy(2, slot, 1, blocks - 2 + slot).wait()
+    slide_copy.wait()
     for copy in swaps + sent:
         copy.wait_send()
 
 
-def project_tiles(tiles, gain, wq, wkv, wo):
+def project_tiles(tiles, gain, wq, wkv, wo, cache, slide_gain, slide_w):
     rows, width = wq.shape
     slots, length, _ = tiles.shape
     count = slots * length
@@ -301,11 +326,12 @@
     one = (2, 2, 3, 4, 4, 2, 4 * rows, 128)
     return pl.pallas_call(
         gather_kernel,
-        in_specs=[vmem, hbm, vmem],
-        out_specs=[hbm, hbm],
+        in_specs=[vmem, hbm, vmem, vmem, vmem, vmem],
+        out_specs=[hbm, hbm, hbm],
         out_shape=[
             jax.ShapeDtypeStruct((3, width // 128, count, 128), jnp.bfloat16),
             jax.ShapeDtypeStruct(one, jnp.bfloat16),
+            jax.ShapeDtypeStruct((cache.shape[0], 3 * 128), jnp.bfloat16),
         ],
         scratch_shapes=[
             pltpu.VMEM((3,) + one, jnp.bfloat16),
@@ -313,6 +339,7 @@
             pltpu.VMEM((2, 6, ROWS, 128), jnp.bfloat16),
             pltpu.VMEM((3, 4 * rows, width // 4), jnp.bfloat16),
             pltpu.VMEM((4, 3, 4 * rows, 128), jnp.bfloat16),
+            pltpu.VMEM((cache.shape[0], 3 * 128), jnp.bfloat16),
             dma((3,)),
             dma((3,)),
             dma((4, 3, 3, 3)),
@@ -322,24 +349,30 @@
             dma((4, 3)),
             dma((2,)),
             dma,
+            dma,
         ],
         compiler_params=pltpu.CompilerParams(
             collective_id=0, has_side_effects=True, vmem_limit_bytes=48 * 1024 * 1024
         ),
         name="gather_project",
-    )(parts, tiles.reshape(count, width), gain)
-
-
-def tile_kernel(live_ref, x_ref, gain_ref, kvq, wo_ref, out_ref, emb_ref, wo, ctx, load):
+    )(parts, tiles.reshape(count, width), gain, cache, slide_gain, slide_w)
+
+
+def tile_kernel(
+    live_ref, x_ref, gain_ref, kvq, wo_ref, proj_ref, out_ref, fresh_ref,
+    wo, proj, emb, ctx, load, proj_load,
+):
     step = pl.program_id(0)
     live = live_ref[0]
     tiles, length, width = x_ref.shape
     pairs = width // 128
     load_copy = pltpu.make_async_copy(wo_ref, wo, load)
+    proj_copy = pltpu.make_async_copy(proj_ref, proj, proj_load)
 
     @pl.when(step == 0)
     def _():
         load_copy.start()
+        proj_copy.start()
 
     @pl.when(step * tiles < live)
     def _():
@@ -389,15 +422,23 @@
 
         lax.fori_loop(0, width // COLS, project_out, 0)
         for t in range(tiles):
-            emb_ref[t] = norm_rows(out_ref[t, 0:16, :], gain_ref[1:2, :])[0:1]
+            emb[pl.ds(step * tiles + t, 1), :] = norm_rows(out_ref[t, 0:16, :], gain_ref[1:2, :])[0:1]
 
     @pl.when(step * tiles >= live)
     def _():
         out_ref[...] = jnp.zeros_like(out_ref)
-        emb_ref[...] = jnp.zeros_like(emb_ref)
-
-
-def encode_tiles(live, tiles, gain, kvq, wo):
+        for t in range(tiles):
+            emb[pl.ds(step * tiles + t, 1), :] = jnp.zeros((1, width), jnp.float32)
+
+    @pl.when(step == pl.num_programs(0) - 1)
+    def _():
+        proj_copy.wait()
+        fresh_ref[...] = jnp.dot(
+            emb[...].astype(jnp.bfloat16), proj[...], preferred_element_type=jnp.float32
+        ).astype(jnp.bfloat16)
+
+
+def encode_tiles(live, tiles, gain, kvq, wo, proj):
     slots, length, width = tiles.shape
     rows = GROUP * length
     return pl.pallas_call(
@@ -410,45 +451,48 @@
                 pl.BlockSpec(memory_space=pltpu.VMEM),
                 pl.BlockSpec((3, width // 128, rows, 128), lambda i, live: (0, 0, i, 0)),
                 pl.BlockSpec(memory_space=pl.ANY),
+                pl.BlockSpec(memory_space=pl.ANY),
             ],
             out_specs=[
                 pl.BlockSpec((GROUP, length, width), lambda i, live: (i, 0, 0)),
-                pl.BlockSpec((GROUP, 1, width), lambda i, live: (i, 0, 0)),
+                pl.BlockSpec((slots, proj.shape[1]), lambda i, live: (0, 0)),
             ],
             scratch_shapes=[
                 pltpu.VMEM((width // 128, width, 128), jnp.bfloat16),
+                pltpu.VMEM(proj.shape, jnp.bfloat16),
+                pltpu.VMEM((slots, width), jnp.float32),
                 pltpu.VMEM((width // 128, rows, 128), jnp.bfloat16),
+                pltpu.SemaphoreType.DMA,
                 pltpu.SemaphoreType.DMA,
             ],
         ),
         out_shape=[
             jax.ShapeDtypeStruct((slots, length, width), jnp.bfloat16),
-            jax.ShapeDtypeStruct((slots, 1, width), jnp.float32),
+            jax.ShapeDtypeStruct((slots, proj.shape[1]), jnp.bfloat16),
         ],
         compiler_params=pltpu.CompilerParams(vmem_limit_bytes=48 * 1024 * 1024),
         name="tile_layer",
-    )(live, tiles, gain, kvq, wo)
+    )(live, tiles, gain, kvq, wo, proj)
 
 
 def slide_kernel(
-    emb_ref, proj_ref, cache_ref, gain_ref, w_ref, live_ref, out_ref,
-    fresh, far, qkv, near, fresh_send, fresh_recv, far_send, far_recv,
+    fresh_ref, cached_ref, cache_ref, gain_ref, w_ref, live_ref, out_ref,
+    fresh, far, qkv, near, fresh_send, fresh_recv, far_send, far_recv, load,
 ):
     seq, head = lax.axis_index("seq"), lax.axis_index("head")
     groups, slots, width = fresh.shape
     seqs = far.shape[0]
-    rows = cache_ref.shape[0]
+    rows = cached_ref.shape[0]
     span = groups * slots
+    load_copy = pltpu.make_async_copy(cached_ref, qkv, load)
+    load_copy.start()
     heads = [(seq, (head + j) % groups) for j in range(1, groups)]
     spots = [((seq + j) % seqs, head) for j in range(1, seqs)]
     barrier = pltpu.get_barrier_semaphore()
     for partner in heads + spots:
         pl.semaphore_signal(barrier, inc=1, device_id=partner, device_id_type=MESH)
 
-    value = jnp.dot(
-        emb_ref[...].astype(jnp.bfloat16), proj_ref[...], preferred_element_type=jnp.float32
-    )
-    fresh[pl.ds(head, 1)] = value.astype(jnp.bfloat16)[None]
+    fresh[pl.ds(head, 1)] = fresh_ref[...][None]
     pl.semaphore_wait(barrier, len(heads) + len(spots))
 
     def fresh_copy(j, slot):
@@ -474,24 +518,15 @@
     for j in range(groups - 1):
         fresh_copy(j, head).start()
 
-    def project(values):
-        normed = norm_rows(values, gain_ref[...]).astype(jnp.bfloat16)
-        return jnp.dot(normed, w_ref[...], preferred_element_type=jnp.float32).astype(jnp.bfloat16)
-
-    def cached(n, _):
-        at = pl.ds(pl.multiple_of(n * 128, 128), 128)
-        qkv[at, :] = project(cache_ref[at, :])
-        return 0
-
-    lax.fori_loop(span // 128, rows // 128, cached, 0)
+    load_copy.wait()
     for j in range(groups - 1):
         fresh_copy(j, (head + groups - 1 - j) % groups).wait_recv()
     mixed = jnp.where(
         live_ref[...] > 0,
         fresh[...].reshape(span, width).astype(jnp.float32),
-        cache_ref[0:span, :].astype(jnp.float32),
+        cache_ref[...].astype(jnp.float32),
     )
-    qkv[0:span, :] = project(mixed)
+    qkv[0:span, :] = project_slide(mixed, gain_ref[...], w_ref)
 
     lane = lax.broadcasted_iota(jnp.int32, (1, 128), 1)
     first = lane < SLIDE_HEAD_SIZE
@@ -563,17 +598,23 @@
         far_copy(j, seq).wait_send()
 
 
-def encode_slide(embedded, proj, cache, gain, weights, live, groups, seqs):
-    slots, width = embedded.shape[0], proj.shape[1]
+def encode_slide(fresh, cached, cache, gain, weights, live, groups, seqs):
+    slots, width = fresh.shape
     rows, columns = cache.shape[0], weights.shape[2]
-    padded = jnp.pad(weights, ((0, 0), (0, 0), (0, 128 - columns)))
-    padded = jnp.transpose(padded, (1, 0, 2)).reshape(width, 3 * 128)
     dma = pltpu.SemaphoreType.DMA
     vmem = pl.BlockSpec(memory_space=pltpu.VMEM)
     return pl.pallas_call(
         slide_kernel,
-        in_specs=[vmem] * 6,
+        in_specs=[
+            vmem,
+            pl.BlockSpec(memory_space=pl.ANY),
+            pl.BlockSpec((groups * slots, width), lambda i: (0, 0)),
+            vmem,
+            vmem,
+            vmem,
+        ],
         out_specs=vmem,
+        grid=(1,),
         out_shape=jax.ShapeDtypeStruct((rows, columns), jnp.bfloat16),
         scratch_shapes=[
             pltpu.VMEM((groups, slots, width), jnp.bfloat16),
@@ -584,12 +625,13 @@
             dma((groups - 1,)),
             dma((seqs - 1,)),
             dma((seqs - 1,)),
+            dma,
         ],
         compiler_params=pltpu.CompilerParams(
             collective_id=1, has_side_effects=True, vmem_limit_bytes=48 * 1024 * 1024
         ),
         name="slide_layer",
-    )(embedded, proj, cache, gain, padded, live)
+    )(fresh, cached, cache, gain, weights, live)
 
 
 def per_device(
@@ -608,17 +650,19 @@
     slot_count = local_tiles.shape[0]
     seq_index = lax.axis_index("seq")
     head_index = lax.axis_index("head")
-    kvq, w_out = project_tiles(local_tiles, tile_gain, tile_wq, tile_wkv, tile_wo)
+    kvq, w_out, cached = project_tiles(
+        local_tiles, tile_gain, tile_wq, tile_wkv, tile_wo, slide_cache, slide_gain[None], slide_qkv
+    )
     w_out = w_out.reshape(kvq.shape[1], -1, 128)
     row_plan = lax.dynamic_index_in_dim(send_map, seq_index, 1, keepdims=False)
     live_count = jnp.sum(row_plan, axis=1)
     own_live = lax.dynamic_slice_in_dim(live_count, head_index, 1, 0)
-    tile_layers, embedded = encode_tiles(own_live, local_tiles, tile_gain, kvq, w_out)
+    tile_layers, fresh = encode_tiles(own_live, local_tiles, tile_gain, kvq, w_out, slide_proj)
     groups, seqs = send_map.shape[0], send_map.shape[1]
     places = jnp.arange(slot_count, dtype=jnp.int32)
     live = (places[None, :] < live_count[:, None]).reshape(groups * slot_count, 1).astype(jnp.float32)
     context = encode_slide(
-        embedded[:, 0], slide_proj, slide_cache, slide_gain[None], slide_qkv, live, groups, seqs
+        fresh, cached, slide_cache, slide_gain[None], slide_qkv, live, groups, seqs
     )
     return (context, tile_layers[None, None])
 

time: 139 us -> 143 us (1.029)
  Pallas kernels: 130 us -> 134 us
    pallas_call x1, Pallas kernels: 12.9 us -> 31.1 us  [encode_tiles(): pl.pallas_call(tile_kernel, grid_spec=pltpu.PrefetchScalarGridSpec(num_sc...]
    pallas_call x2, Pallas kernels: 117 us -> 102 us  [the longest x1 83.8 us: project_tiles(): pl.pallas_call(gather_kernel, in_specs=[vmem, hbm, vmem, vmem, vmem, vmem...]
    unnamed x14 -> x12, local copies, waits for them, and re-layouts: 3.78 us -> 5.09 us
where the time goes in v5:
time: 143 us; the launch traced here: 142 us
  Pallas kernels  134 us (94%)
  local copies, waits for them, and re-layouts  6.62 us (5%)
    pallas_call x1, Pallas kernels, project_tiles(): pl.pallas_call(gather_kernel, in_specs=[vmem, hbm, vmem, vmem, vmem, vmem...  83.8 us
    pallas_call x1, Pallas kernels, encode_tiles(): pl.pallas_call(tile_kernel, grid_spec=pltpu.PrefetchScalarGridSpec(num_sc...  31.1 us
    pallas_call x1, Pallas kernels, encode_slide(): pl.pallas_call(slide_kernel, in_specs=[vmem, pl.BlockSpec(memory_space=pl...  18.7 us
    unnamed x12, local copies, waits for them, and re-layouts  5.09 us

profile of v5, /device:TPU:0, one launch (start us, length us, event | category | flops | bytes accessed | tf_op | source)
XLA Modules:
  0.0 142.2 jit_solution(819971940171547863)
XLA Ops:
  0.6 0.0 copy-start
  0.6 0.8 copy-done
  1.5 0.2 dynamic-slice_reduce_fusion
  1.7 0.6 dynamic_slice.8.live_ref
  2.3 1.3 copy.19.slide_w_ref.w_ref
  3.6 0.7 broadcast_in_dim.4.slide_gain_ref.gain_ref
  4.3 1.0 pad_maximum_fusion
  5.3 0.1 reshape.42
  5.4 0.1 copy.17
  5.5 0.0 copy-start.1
  5.5 1.4 copy-done.1
  6.9 0.0 copy-start.4
  6.9 0.7 copy-done.4
  7.6 0.0 copy-start.3
  7.6 83.8 %gather_project.1 = (bf16[3,12,2048,128]{3,2,1,0:T(8,128)(2,1)}, bf16[2,2,3,4,4,2,48,128]{7,6,5,4,3,2,1,0:T(8,128)(2,1)}, bf16[1024,384]{1,0:T(8,128)(2,1)S(1)}) custom-call(bf16[4,48,384]{2,1,0:T(8,128)(2,1)S(1)} %copy.18.w_ref, bf16[2048,1536]{1,0:T(8,128)(2,1)} %bitcast.7, f32[2,1536]{1,0:T(2,128)S(1)} %copy-done.4, bf16[1024,768]{1,0:T(8,128)(2,1)S(1)} %copy-done.1, ...), custom_call_target="tpu_custom_call" | custom-call | tf_op jit(solution)/shard_map/gather_project/pallas_call | solution.py:327
  91.4 0.0 copy-done.3
  91.4 0.0 copy-start.2
  91.4 31.1 %tile_layer.1 = (bf16[16,128,1536]{2,1,0:T(8,128)(2,1)}, bf16[16,768]{1,0:T(8,128)(2,1)S(1)}) custom-call(s32[1]{0:T(128)} %dynamic_slice.8.live_ref, bf16[16,128,1536]{2,1,0:T(8,128)(2,1)} %bitcast.8, f32[2,1536]{1,0:T(2,128)S(1)} %copy-done.4, bf16[3,12,2048,128]{3,2,1,0:T(8,128)(2,1)} %get-tuple-element.7.kvq, bf16[12,1536,128]{2,1,0:T(8,128)(2,1)} %bitcast.9, ...), custom_call_target="tpu_custom_call" | custom-call | tf_op jit(solution)/shard_map/tile_layer/pallas_call | solution.py:444
  122.5 0.1 fusion
  122.6 0.1 reshape.46.live_ref
  122.7 0.0 copy-done.2
  122.7 18.7 %slide_layer.1 = bf16[1024,96]{1,0:T(8,128)(2,1)S(1)} custom-call(bf16[16,768]{1,0:T(8,128)(2,1)S(1)} %get-tuple-element.9.fresh_ref, bf16[1024,384]{1,0:T(8,128)(2,1)S(1)} %get-tuple-element.10.cached_ref, bf16[1024,768]{1,0:T(8,128)(2,1)S(1)} %copy-done.2, f32[1,768]{1,0:T(1,128)S(1)} %broadcast_in_dim.4.slide_gain_ref.gain_ref, ...), custom_call_target="tpu_custom_call" | custom-call | tf_op jit(solution)/shard_map/slide_layer/pallas_call | solution.py:606
  141.3 0.8 copy.22
  (1 shorter events, 0.0 us)
Async XLA Ops:
  0.6 0.8 copy-start
  5.5 1.4 copy-start.1
  6.9 0.7 copy-start.4
  7.6 83.8 %copy-start.3 = (bf16[1536,768]{1,0:T(8,128)(2,1)S(1)}, bf16[1536,768]{1,0:T(8,128)(2,1)}, u32[]{:S(2)}) copy-start(bf16[1536,768]{1,0:T(8,128)(2,1)} %proj_ref.1) | copy-start | bytes 7077892
  91.4 31.3 %copy-start.2 = (bf16[1024,768]{1,0:T(8,128)(2,1)S(1)}, bf16[1024,768]{1,0:T(8,128)(2,1)}, u32[]{:S(2)}) copy-start(bf16[1024,768]{1,0:T(8,128)(2,1)} %cache_ref.3) | copy-start | bytes 4718596

commit v6 on v4

--- a/solution.py
+++ b/solution.py
@@ -16,7 +16,7 @@
 MESH = pl.DeviceIdType.MESH
 ORDERS = (("x", "y", "z"), ("y", "z", "x"), ("z", "x", "y"))
 RING = 4
-ROWS = 512
+ROWS = 1024
 
 
 def norm_rows(values, gain):
@@ -74,7 +74,7 @@
 
     def normalise(start, count):
         def step(r, _):
-            at = pl.ds(pl.multiple_of(r * 32, 32), 32)
+            at = pl.ds(pl.multiple_of(r * 64, 64), 64)
             rows_ref[at, :] = norm_rows(rows_ref[at, :], gain_ref[0:1, :]).astype(jnp.bfloat16)
             return 0
 
@@ -141,9 +141,7 @@
             )
         )
         swaps[n].start()
-    load_copy.wait()
-    share = -(-length // 32 // 6)
-    normalise(0, share)
+    share = -(-length // 64 // 5)
     for n in range(3):
         swaps[n].wait_recv()
     count = 4 * 48
@@ -215,10 +213,10 @@
         keeps.append(copy)
     for copy in keeps:
         copy.wait()
-    done = [share]
+    done = [0]
 
     def norm_some():
-        count = min(share, length // 32 - done[0])
+        count = min(share, length // 64 - done[0])
         normalise(done[0], count)
         done[0] += count
 
@@ -254,6 +252,7 @@
         for p in range(3):
             step(m, p, *rest)
 
+    load_copy.wait()
     norm_some()
     for phase in range(2):
         for m in range(4):

time: 139 us -> 136 us (0.978)
  Pallas kernels: 130 us -> 127 us
    pallas_call x1, Pallas kernels: 35.8 us -> 18.2 us  [encode_slide(): pl.pallas_call(slide_kernel, in_specs=[vmem] * 6, out_specs=vmem, out_sha...]
    pallas_call x1, Pallas kernels: 12.9 us -> 29.7 us  [encode_tiles(): pl.pallas_call(tile_kernel, grid_spec=pltpu.PrefetchScalarGridSpec(num_sc...]
    pallas_call x1, Pallas kernels: 81.2 us -> 79 us  [project_tiles(): pl.pallas_call(gather_kernel, in_specs=[vmem, hbm, vmem], out_specs=[hbm,...]
where the time goes in v6:
time: 136 us
  Pallas kernels  127 us (93%)
  local copies, waits for them, and re-layouts  6.85 us (5%)
    pallas_call x1, Pallas kernels, project_tiles(): pl.pallas_call(gather_kernel, in_specs=[vmem, hbm, vmem], out_specs=[hbm,...  79 us
    pallas_call x1, Pallas kernels, encode_tiles(): pl.pallas_call(tile_kernel, grid_spec=pltpu.PrefetchScalarGridSpec(num_sc...  29.7 us
    pallas_call x1, Pallas kernels, encode_slide(): pl.pallas_call(slide_kernel, in_specs=[vmem] * 6, out_specs=vmem, out_sha...  18.2 us
    unnamed x14, local copies, waits for them, and re-layouts  3.78 us

profile of v6, /device:TPU:0, one launch (start us, length us, event | category | flops | bytes accessed | tf_op | source)
XLA Modules:
  0.0 135.8 jit_solution(261421864797497840)
XLA Ops:
  0.6 0.0 copy-start
  0.6 0.8 copy-done
  1.5 0.2 dynamic-slice_reduce_fusion
  1.7 0.6 dynamic_slice.8.live_ref
  2.3 1.0 pad_maximum_fusion
  3.3 0.1 reshape.45
  3.4 0.1 copy.16
  3.5 0.0 copy-start.3
  3.5 0.7 copy-done.3
  4.2 79.0 %gather_project.1 = (bf16[3,12,2048,128]{3,2,1,0:T(8,128)(2,1)}, bf16[2,2,3,4,4,2,48,128]{7,6,5,4,3,2,1,0:T(8,128)(2,1)S(1)}) custom-call(bf16[4,48,384]{2,1,0:T(8,128)(2,1)S(1)} %copy.17.w_ref, bf16[2048,1536]{1,0:T(8,128)(2,1)} %bitcast.15, f32[2,1536]{1,0:T(2,128)S(1)} %copy-done.3), custom_call_target="tpu_custom_call" | custom-call | tf_op jit(solution)/shard_map/gather_project/pallas_call | solution.py:301
  83.2 0.0 copy-start.4
  83.2 0.0 copy-start.5
  83.2 0.0 copy-start.1
  83.2 29.7 %tile_layer.1 = (bf16[16,128,1536]{2,1,0:T(8,128)(2,1)}, f32[16,1,1536]{2,1,0:T(1,128)S(1)}) custom-call(s32[1]{0:T(128)} %dynamic_slice.8.live_ref, bf16[16,128,1536]{2,1,0:T(8,128)(2,1)} %bitcast.16, f32[2,1536]{1,0:T(2,128)S(1)} %copy-done.3, bf16[3,12,2048,128]{3,2,1,0:T(8,128)(2,1)} %get-tuple-element.6.kvq, bf16[12,1536,128]{2,1,0:T(8,128)(2,1)S(1)} %bitcast.13), custom_call_target="tpu_custom_call" | custom-call | tf_op jit(solution)/shard_map/tile_layer/pallas_call | solution.py:402
  112.9 0.1 fusion
  113.0 0.1 reshape.50.live_ref
  113.1 0.0 copy-done.4
  113.1 0.9 pad.4
  114.0 1.4 %copy.18.w_ref = bf16[768,384]{1,0:T(8,128)(2,1)S(1)} copy(bf16[768,384]{0,1:T(8,128)(2,1)} %bitcast.17) | data formatting | bytes 1179648 | tf_op jit(solution)/shard_map/reshape | solution.py:569
  115.3 0.0 copy-done.5
  115.4 0.0 copy-done.1
  115.4 0.0 copy-start.2
  115.4 1.4 %copy-done.2 = bf16[1024,768]{1,0:T(8,128)(2,1)S(1)} copy-done((bf16[1024,768]{1,0:T(8,128)(2,1)S(1)}, bf16[1024,768]{1,0:T(8,128)(2,1)}, u32[]{:S(2)}) %copy-start.2) | copy-done | bytes 1572888
  116.8 18.2 %slide_layer.1 = bf16[1024,96]{1,0:T(8,128)(2,1)S(1)} custom-call(f32[16,1536]{1,0:T(8,128)S(1)} %bitcast.14, bf16[1536,768]{1,0:T(8,128)(2,1)S(1)} %copy-done.1, bf16[1024,768]{1,0:T(8,128)(2,1)S(1)} %copy-done.2, f32[1,768]{1,0:T(1,128)S(1)} %broadcast_in_dim.8.gain_ref, bf16[768,384]{1,0:T(8,128)(2,1)S(1)} %copy.18.w_ref, f32[128,1]{1,0:T(8,128)S(1)} %reshape.50.live_ref), custom_call_target="tpu_custom_call" | custom-call | tf_op jit(solution)/shard_map/slide_layer/pallas_call | solution.py:572
  135.0 0.8 copy.20
  (3 shorter events, 0.0 us)
Async XLA Ops:
  0.6 0.8 copy-start
  3.5 0.7 copy-start.3
  83.2 29.9 %copy-start.4 = (bf16[3,768,96]{1,2,0:T(8,128)(2,1)S(1)}, bf16[3,768,96]{1,2,0:T(8,128)(2,1)}, u32[]{:S(2)}) copy-start(bf16[3,768,96]{1,2,0:T(8,128)(2,1)} %param.18) | copy-start | bytes 1327108
  83.2 32.2 %copy-start.5 = (f32[768]{0:T(1024)S(1)}, f32[768]{0:T(1024)}, u32[]{:S(2)}) copy-start(f32[768]{0:T(1024)} %param.17) | copy-start | bytes 9220
  83.2 32.2 %copy-start.1 = (bf16[1536,768]{1,0:T(8,128)(2,1)S(1)}, bf16[1536,768]{1,0:T(8,128)(2,1)}, u32[]{:S(2)}) copy-start(bf16[1536,768]{1,0:T(8,128)(2,1)} %proj_ref.1) | copy-start | bytes 7077892
  115.4 1.4 %copy-start.2 = (bf16[1024,768]{1,0:T(8,128)(2,1)S(1)}, bf16[1024,768]{1,0:T(8,128)(2,1)}, u32[]{:S(2)}) copy-start(bf16[1024,768]{1,0:T(8,128)(2,1)} %cache_ref.1) | copy-start | bytes 4718596

commit v7 on v6

--- a/solution.py
+++ b/solution.py
@@ -263,9 +263,9 @@
         norm_some()
     every(first_arrivals, 0, 2)
     every(start_phase, 2, 2)
-    every(last_arrival, 0, 2)
     every(first_arrivals, 1, 2)
     every(start_phase, 3, 2)
+    every(last_arrival, 0, 2)
     every(from_pair, 0)
     multiply(0, 0, blocks)
     every(last_arrival, 1, 2)

time: 136 us -> 135 us (level)
    pallas_call x1, Pallas kernels: 29.7 us -> 12.9 us  [encode_tiles(): pl.pallas_call(tile_kernel, grid_spec=pltpu.PrefetchScalarGridSpec(num_sc...]
    pallas_call x1, Pallas kernels: 18.2 us -> 34.4 us  [encode_slide(): pl.pallas_call(slide_kernel, in_specs=[vmem] * 6, out_specs=vmem, out_sha...]
where the time goes in v7:
time: 135 us
  Pallas kernels  126 us (93%)
  local copies, waits for them, and re-layouts  6.85 us (5%)
    pallas_call x1, Pallas kernels, project_tiles(): pl.pallas_call(gather_kernel, in_specs=[vmem, hbm, vmem], out_specs=[hbm,...  78.9 us
    pallas_call x1, Pallas kernels, encode_slide(): pl.pallas_call(slide_kernel, in_specs=[vmem] * 6, out_specs=vmem, out_sha...  34.4 us
    pallas_call x1, Pallas kernels, encode_tiles(): pl.pallas_call(tile_kernel, grid_spec=pltpu.PrefetchScalarGridSpec(num_sc...  12.9 us
    unnamed x14, local copies, waits for them, and re-layouts  3.78 us

profile of v7, /device:TPU:0, one launch (start us, length us, event | category | flops | bytes accessed | tf_op | source)
XLA Modules:
  0.0 135.2 jit_solution(2477715695431595654)
XLA Ops:
  0.6 0.0 copy-start
  0.6 0.8 copy-done
  1.5 0.2 dynamic-slice_reduce_fusion
  1.7 0.6 dynamic_slice.8.live_ref
  2.3 1.0 pad_maximum_fusion
  3.3 0.1 reshape.45
  3.4 0.1 copy.16
  3.5 0.0 copy-start.3
  3.5 0.7 copy-done.3
  4.2 78.9 %gather_project.1 = (bf16[3,12,2048,128]{3,2,1,0:T(8,128)(2,1)}, bf16[2,2,3,4,4,2,48,128]{7,6,5,4,3,2,1,0:T(8,128)(2,1)S(1)}) custom-call(bf16[4,48,384]{2,1,0:T(8,128)(2,1)S(1)} %copy.17.w_ref, bf16[2048,1536]{1,0:T(8,128)(2,1)} %bitcast.15, f32[2,1536]{1,0:T(2,128)S(1)} %copy-done.3), custom_call_target="tpu_custom_call" | custom-call | tf_op jit(solution)/shard_map/gather_project/pallas_call | solution.py:301
  83.1 0.0 copy-start.4
  83.1 0.0 copy-start.5
  83.1 0.0 copy-start.1
  83.1 12.9 %tile_layer.1 = (bf16[16,128,1536]{2,1,0:T(8,128)(2,1)}, f32[16,1,1536]{2,1,0:T(1,128)S(1)}) custom-call(s32[1]{0:T(128)} %dynamic_slice.8.live_ref, bf16[16,128,1536]{2,1,0:T(8,128)(2,1)} %bitcast.16, f32[2,1536]{1,0:T(2,128)S(1)} %copy-done.3, bf16[3,12,2048,128]{3,2,1,0:T(8,128)(2,1)} %get-tuple-element.6.kvq, bf16[12,1536,128]{2,1,0:T(8,128)(2,1)S(1)} %bitcast.13), custom_call_target="tpu_custom_call" | custom-call | tf_op jit(solution)/shard_map/tile_layer/pallas_call | solution.py:402
  96.1 0.1 fusion
  96.2 0.1 reshape.50.live_ref
  96.2 0.0 copy-done.4
  96.3 0.9 pad.4
  97.1 1.4 %copy.18.w_ref = bf16[768,384]{1,0:T(8,128)(2,1)S(1)} copy(bf16[768,384]{0,1:T(8,128)(2,1)} %bitcast.17) | data formatting | bytes 1179648 | tf_op jit(solution)/shard_map/reshape | solution.py:569
  98.5 0.0 copy-done.5
  98.5 0.0 copy-done.1
  98.5 0.0 copy-start.2
  98.5 1.4 %copy-done.2 = bf16[1024,768]{1,0:T(8,128)(2,1)S(1)} copy-done((bf16[1024,768]{1,0:T(8,128)(2,1)S(1)}, bf16[1024,768]{1,0:T(8,128)(2,1)}, u32[]{:S(2)}) %copy-start.2) | copy-done | bytes 1572888
  99.9 34.4 %slide_layer.1 = bf16[1024,96]{1,0:T(8,128)(2,1)S(1)} custom-call(f32[16,1536]{1,0:T(8,128)S(1)} %bitcast.14, bf16[1536,768]{1,0:T(8,128)(2,1)S(1)} %copy-done.1, bf16[1024,768]{1,0:T(8,128)(2,1)S(1)} %copy-done.2, f32[1,768]{1,0:T(1,128)S(1)} %broadcast_in_dim.8.gain_ref, bf16[768,384]{1,0:T(8,128)(2,1)S(1)} %copy.18.w_ref, f32[128,1]{1,0:T(8,128)S(1)} %reshape.50.live_ref), custom_call_target="tpu_custom_call" | custom-call | tf_op jit(solution)/shard_map/slide_layer/pallas_call | solution.py:572
  134.3 0.8 copy.20
  (3 shorter events, 0.0 us)
Async XLA Ops:
  0.6 0.8 copy-start
  3.5 0.7 copy-start.3
  83.1 13.2 %copy-start.4 = (bf16[3,768,96]{1,2,0:T(8,128)(2,1)S(1)}, bf16[3,768,96]{1,2,0:T(8,128)(2,1)}, u32[]{:S(2)}) copy-start(bf16[3,768,96]{1,2,0:T(8,128)(2,1)} %param.18) | copy-start | bytes 1327108
  83.1 15.4 %copy-start.5 = (f32[768]{0:T(1024)S(1)}, f32[768]{0:T(1024)}, u32[]{:S(2)}) copy-start(f32[768]{0:T(1024)} %param.17) | copy-start | bytes 9220
  83.1 15.4 %copy-start.1 = (bf16[1536,768]{1,0:T(8,128)(2,1)S(1)}, bf16[1536,768]{1,0:T(8,128)(2,1)}, u32[]{:S(2)}) copy-start(bf16[1536,768]{1,0:T(8,128)(2,1)} %proj_ref.1) | copy-start | bytes 7077892
  98.5 1.4 %copy-start.2 = (bf16[1024,768]{1,0:T(8,128)(2,1)S(1)}, bf16[1024,768]{1,0:T(8,128)(2,1)}, u32[]{:S(2)}) copy-start(bf16[1024,768]{1,0:T(8,128)(2,1)} %cache_ref.1) | copy-start | bytes 4718596
